TPU v7x, 32 devices: a whole 2x2x4 slice. The times are simulated.
32 devices in a mesh: ctx: 8 (over y, x, core), tp: 4 (over z).
Axes of the slice: x: 2, y: 2, z: 4, core: 2. Of those that a mesh axis runs over, the one named last changes fastest.
Arguments:
- query: bfloat16 [8192, 4096], P('ctx', 'tp'), may hold values from -6 to 6
- keys: bfloat16 [8192, 4096], P('ctx', 'tp'), may hold values from -6 to 6
- values: bfloat16 [8192, 4096], P('ctx', 'tp'), may hold values from -6 to 6
- residues: float32 [256, 16], replicated, may hold values from -1.5 to 1.5
- rates: float32 [256, 16], replicated, as said below
- w_out: bfloat16 [4096, 4096], P('tp'), may hold values from -0.125 to 0.125
Outputs:
- mixed: bfloat16 [8192, 4096], P('ctx', 'tp')
Inputs may be any that keep to these rules, and one draw needn't show every extreme that they name: `rates`: each rate lies between 0.25 / 8192 and 1 / 32.
All inputs are finite; a program needn't handle non-finite values.
Results may differ from a plain program's by a relative error of at most 0.015.
Values may be sent and summed in bfloat16 or wider, within the bound.
A program may use at most 128 MiB of HBM per device.

v0:
```python
import functools
import math

import jax
import jax.numpy as jnp
from jax import lax
from jax.experimental import pallas as pl
from jax.experimental.pallas import tpu as pltpu
from jax.sharding import PartitionSpec as P

SHARE = 16
LANES = 128
MESH = pl.DeviceIdType.MESH
F32 = jnp.float32
BF16 = jnp.bfloat16


def split(x):
    upper = x.astype(BF16)
    return upper, (x - upper.astype(F32)).astype(BF16)


def dot(a, b):
    return jnp.dot(a, b, preferred_element_type=F32)


def conv_kernel(ctx, state, chunk, q_ref, k_ref, v_ref, rrow_ref, grow_ref, rcol_ref, rlane_ref, gmask_ref,
                smask_ref, out_ref, states, own, before, inside, wide, taps, carry, send_sem, recv_sem):
    block, width = q_ref.shape
    chunks = block // chunk
    lane_blocks = width // LANES
    groups = LANES // SHARE
    modes = groups * state
    me = lax.axis_index("ctx")

    barrier = pltpu.get_barrier_semaphore()

    def greet(d, _):
        pl.semaphore_signal(barrier, inc=1, device_id={"ctx": lax.rem(me + d, ctx)}, device_id_type=MESH)
        return 0

    lax.fori_loop(1, ctx, greet, 0)

    def product(k, lanes):
        rows = pl.ds(k * chunk, chunk)
        return (k_ref[rows, lanes].astype(F32) * v_ref[rows, lanes].astype(F32)).astype(BF16)

    def lanes_of(b):
        return pl.ds(pl.multiple_of(b * LANES, LANES), LANES)

    def rates_col(b):
        return rcol_ref[pl.ds(pl.multiple_of(b * modes, modes), modes), :]

    def state_step(b, _):
        lanes = lanes_of(b)
        tau = lax.broadcasted_iota(jnp.int32, (modes, chunk), 1).astype(F32)
        upper, lower = split(jnp.exp(-rates_col(b) * (chunk - 1.0 - tau)))
        decay = jnp.exp(-rlane_ref[:, lanes] * float(chunk))
        gmask = gmask_ref[...]
        total = jnp.zeros((state, LANES), F32)
        for k in range(chunks):
            x = product(k, lanes)
            fresh = (dot(upper, x) + dot(lower, x)) * gmask
            before[k, :, lanes] = total
            total = total * decay + fresh.reshape(groups, state, LANES).sum(0)
        own[:, lanes] = total
        return 0

    lax.fori_loop(0, lane_blocks, state_step, 0)

    pl.semaphore_wait(barrier, ctx - 1)

    def to_peer(d):
        return pltpu.make_async_remote_copy(
            src_ref=own, dst_ref=states.at[me], send_sem=send_sem.at[d], recv_sem=recv_sem.at[me],
            device_id={"ctx": lax.rem(me + d, ctx)}, device_id_type=MESH)

    def from_peer(j):
        return pltpu.make_async_remote_copy(
            src_ref=own, dst_ref=states.at[j], send_sem=send_sem.at[0], recv_sem=recv_sem.at[j],
            device_id={"ctx": j}, device_id_type=MESH)

    lax.fori_loop(1, ctx - me, lambda d, _: (to_peer(d).start(), 0)[1], 0)

    def inside_step(b, _):
        lanes = lanes_of(b)
        row = lax.broadcasted_iota(jnp.int32, (chunk, modes), 0).astype(F32)
        col = lax.broadcasted_iota(jnp.int32, (modes, chunk), 1).astype(F32)
        middle = chunk / 2.0
        falling = grow_ref[pl.ds(b, 1), :] * jnp.exp(-rrow_ref[pl.ds(b, 1), :] * (row - middle))
        b_hi, b_lo = split(jnp.exp(rates_col(b) * (col - middle)))
        causal = lax.broadcasted_iota(jnp.int32, (chunk, chunk), 0) >= lax.broadcasted_iota(
            jnp.int32, (chunk, chunk), 1)
        xs = [product(k, lanes) for k in range(chunks)]
        for g in range(groups):
            a_hi, a_lo = split(falling * smask_ref[g:g + 1, :])
            tap = dot(a_hi, b_hi) + dot(a_lo, b_hi) + dot(a_hi, b_lo)
            taps[:, g * chunk:(g + 1) * chunk] = jnp.where(causal, tap, 0.0).astype(BF16)
            only = gmask_ref[g * state:g * state + 1, :].astype(BF16)
            for k in range(chunks):
                wide[g * chunk:(g + 1) * chunk, k * LANES:(k + 1) * LANES] = xs[k] * only
        inside[b] = dot(taps[...], wide[...])
        return 0

    lax.fori_loop(0, lane_blocks, inside_step, 0)

    lax.fori_loop(0, me, lambda j, _: (from_peer(j).wait_recv(), 0)[1], 0)

    def carry_step(b, _):
        lanes = lanes_of(b)
        rlane = rlane_ref[:, lanes]
        hop = jnp.exp(-rlane * float(block))
        decay = jnp.exp(-rlane * float(chunk))
        reached = lax.fori_loop(
            0, me, lambda j, r: r * hop + states[j, :, lanes], jnp.zeros((state, LANES), F32))
        gmask = gmask_ref[...]
        for k in range(chunks):
            entering = before[k, :, lanes] + reached
            reached = reached * decay
            spread = jnp.concatenate([entering] * groups, axis=0) * gmask
            hi, lo = split(spread)
            at = slice(k * LANES, (k + 1) * LANES)
            carry[0:modes, at] = hi
            carry[modes:2 * modes, at] = hi
            carry[2 * modes:3 * modes, at] = lo
        row = lax.broadcasted_iota(jnp.int32, (chunk, modes), 0).astype(F32)
        hi, lo = split(grow_ref[pl.ds(b, 1), :] * jnp.exp(-rrow_ref[pl.ds(b, 1), :] * (row + 1.0)))
        full = inside[b] + dot(jnp.concatenate([hi, lo, hi], axis=1), carry[...])
        for k in range(chunks):
            rows = pl.ds(k * chunk, chunk)
            convolved = full[:, k * LANES:(k + 1) * LANES].astype(BF16)
            out_ref[rows, lanes] = (q_ref[rows, lanes].astype(F32) * convolved.astype(F32)).astype(BF16)
        return 0

    lax.fori_loop(0, lane_blocks, carry_step, 0)
    lax.fori_loop(1, ctx - me, lambda d, _: (to_peer(d).wait_send(), 0)[1], 0)


def gated_conv(query, keys, values, rates, gain, ctx):
    block, width = keys.shape
    state = rates.shape[1]
    chunk = math.gcd(block, LANES)
    chunks = block // chunk
    groups = LANES // SHARE
    modes = groups * state
    lane_blocks = width // LANES
    rows = jnp.arange(modes)[:, None] // state
    gmask = (rows == jnp.arange(LANES)[None, :] // SHARE).astype(F32)
    smask = (jnp.arange(groups)[:, None] == jnp.arange(modes)[None, :] // state).astype(F32)
    vmem = pl.BlockSpec(memory_space=pltpu.VMEM)
    return pl.pallas_call(
        functools.partial(conv_kernel, ctx, state, chunk),
        out_shape=jax.ShapeDtypeStruct((block, width), BF16),
        in_specs=[vmem] * 9,
        out_specs=vmem,
        scratch_shapes=[
            pltpu.VMEM((ctx, state, width), F32),
            pltpu.VMEM((state, width), F32),
            pltpu.VMEM((chunks, state, width), F32),
            pltpu.VMEM((lane_blocks, chunk, chunks * LANES), F32),
            pltpu.VMEM((groups * chunk, chunks * LANES), BF16),
            pltpu.VMEM((chunk, groups * chunk), BF16),
            pltpu.VMEM((3 * modes, chunks * LANES), BF16),
            pltpu.SemaphoreType.DMA((ctx,)),
            pltpu.SemaphoreType.DMA((ctx,)),
        ],
        compiler_params=pltpu.CompilerParams(
            collective_id=0, has_side_effects=True, vmem_limit_bytes=40 * 2**20),
        cost_estimate=pl.CostEstimate(
            flops=40 * block * width * chunk, bytes_accessed=8 * block * width, transcendentals=0),
        name="gated_conv",
    )(query, keys, values, rates.reshape(lane_blocks, modes), gain.reshape(lane_blocks, modes),
      rates.reshape(lane_blocks * modes, 1), jnp.repeat(rates.T, SHARE, axis=1), gmask, smask)


def on_device(ctx, tp, query, keys, values, residues, rates, w_out):
    width = keys.shape[1]
    groups = width // SHARE
    place = lax.axis_index("tp")
    rates = lax.dynamic_slice_in_dim(rates, place * groups, groups, 0)
    residues = lax.dynamic_slice_in_dim(residues, place * groups, groups, 0)
    gain = residues * jnp.sqrt(2.0 * rates)
    gated = gated_conv(query, keys, values, rates, gain, ctx)
    mixed = dot(gated, w_out).astype(BF16)
    return lax.psum_scatter(mixed, "tp", scatter_dimension=1, tiled=True)


def solution(mesh):
    in_specs = (P("ctx", "tp"), P("ctx", "tp"), P("ctx", "tp"), P(), P(), P("tp", None))
    return jax.shard_map(
        functools.partial(on_device, mesh.shape["ctx"], mesh.shape["tp"]),
        mesh=mesh, in_specs=in_specs, out_specs=P("ctx", "tp"), check_vma=False)
```

profile of v0, /device:TPU:14, one launch (start us, length us, event | category | flops | bytes accessed | tf_op | source)
XLA Modules:
  0.0 192.5 jit_solution(10294842678853424658)
XLA Ops:
  6.5 0.0 reduce-scatter.2.cloned.1.call-start
  6.5 0.1 compare_convert_fusion.gmask_ref
  6.6 0.8 sqrt_multiply_fusion
  7.4 0.1 copy.10
  7.5 0.1 reshape.86.rrow_ref
  7.6 0.3 reshape.90.rcol_ref
  7.9 0.1 copy.11
  8.0 0.1 reshape.87.grow_ref
  8.1 0.2 broadcast_in_dim.2
  8.3 0.3 reshape.89.rlane_ref
  8.5 0.0 copy-start
  8.6 1.6 copy-done
  10.1 0.0 copy-start.1
  10.1 1.6 copy-done.1
  11.7 0.0 copy-start.2
  11.7 1.6 copy-done.2
  13.3 0.0 copy-start.3
  13.3 16.0 %gated_conv.1 = bf16[1024,1024]{1,0:T(8,128)(2,1)S(1)} custom-call(bf16[1024,1024]{1,0:T(8,128)(2,1)S(1)} %copy-done, bf16[1024,1024]{1,0:T(8,128)(2,1)S(1)} %copy-done.1, bf16[1024,1024]{1,0:T(8,128)(2,1)S(1)} %copy-done.2, f32[8,128]{1,0:T(8,128)S(1)} %reshape.86.rrow_ref, f32[8,128]{1,0:T(8,128)S(1)} %reshape.87.grow_ref, ...), custom_call_target="tpu_custom_call" | custom-call | flops 5368709120 | bytes 8388608 | tf_op jit(solution)/shard_map/gated_conv/pallas_call | solution.py:151
  29.3 0.0 copy-done.3
  29.3 10.8 %convolution_convert_fusion = bf16[1024,4096]{1,0:T(8,128)(2,1)} fusion(bf16[1024,1024]{1,0:T(8,128)(2,1)S(1)} %gated_conv.1, bf16[1024,4096]{1,0:T(8,128)(2,1)S(1)} %copy-done.3), kind=kOutput, calls=%fused_computation | convolution fusion | flops 8594128896 | bytes 18874368 | tf_op jit(solution)/shard_map/dot_general | solution.py:24
  40.2 0.0 reduce-scatter.2.cloned.1.call-update
  40.2 145.4 %reduce-scatter.2.cloned.1.call-done = bf16[1024,1024]{1,0:T(8,128)(2,1)} async-done(((bf16[1024,4096]{1,0:T(8,128)(2,1)}), bf16[1024,1024]{1,0:T(8,128)(2,1)}) %reduce-scatter.2.cloned.1.call-update) | async-done | bytes 2097168 | tf_op jit(solution)/shard_map/reduce_scatter | solution.py:185
  (2 shorter events, 0.0 us)
Async XLA Ops:
  6.5 179.1 %reduce-scatter.2.cloned.1.call-start = ((), (), s32[]{:S(2)}) async-start(), calls=%async_computation.1 | async-start | bytes 10485760 | tf_op jit(solution)/shard_map/reduce_scatter | solution.py:185
  8.5 1.6 copy-start
  10.1 1.6 copy-start.1
  11.7 1.6 copy-start.2
  13.3 16.0 %copy-start.3 = (bf16[1024,4096]{1,0:T(8,128)(2,1)S(1)}, bf16[1024,4096]{1,0:T(8,128)(2,1)}, u32[]{:S(2)}) copy-start(bf16[1024,4096]{1,0:T(8,128)(2,1)} %param.11) | copy-start | bytes 25165828
Sparse Core Ops, SparseCore 0:
  40.3 145.2 reduce-scatter.1
where the time goes:
time: 195 us; the launch traced here: 192 us
  waiting for transfers between devices  145 us (74%)
  Pallas kernels  16 us (8%)
  between operations  13.4 us (7%)
  matrix products  10.8 us (6%)
  local copies, waits for them, and re-layouts  5.86 us (3%)
    reduce_scatter x1, waiting for transfers between devices, on_device(): return lax.psum_scatter(mixed, 'tp', scatter_dimension=1, tiled=True)  145 us
    pallas_call x1, Pallas kernels, gated_conv(): pl.pallas_call(functools.partial(conv_kernel, ctx, state, chunk), out_sha...  16 us
    dot_general x1, matrix products, dot(): return jnp.dot(a, b, preferred_element_type=F32)  10.8 us
    unnamed x8, local copies, waits for them, and re-layouts  4.77 us
  transfers between devices with their start and end apart: 1, of which 1 were waited for; matrix products, arithmetic and copies ran while one was open for 0% of the time, Pallas kernels for 0%

commit v1 on v0

--- a/solution.py
+++ b/solution.py
@@ -173,16 +173,249 @@
       rates.reshape(lane_blocks * modes, 1), jnp.repeat(rates.T, SHARE, axis=1), gmask, smask)
 
 
+def project_kernel(ctx, tp, tiles, gated_ref, w_hbm, *rest):
+    slices = rest[:tp - 1]
+    (out_ref, w_ref, columns, right_buf, left_buf, part, w_sem, own_sem, spread_send, spread_recv,
+     right_send, right_recv, left_send, left_recv) = rest[tp - 1:]
+    block, width = gated_ref.shape
+    rows = block // (2 * tiles)
+    piece = slices[0].shape[0]
+    place = lax.axis_index("tp")
+    far = tp - 1 - place
+    me = lax.axis_index("ctx")
+    has_left = place > 0
+    has_right = place < tp - 1
+
+    w_copy = pltpu.make_async_copy(w_hbm, w_ref, w_sem)
+    w_copy.start()
+
+    barrier = pltpu.get_barrier_semaphore()
+
+    def greet(d, _):
+        pl.semaphore_signal(barrier, inc=1, device_id={"ctx": lax.rem(me + d, ctx)}, device_id_type=MESH)
+        return 0
+
+    lax.fori_loop(1, ctx, greet, 0)
+
+    @pl.when(has_left)
+    def _():
+        pl.semaphore_signal(barrier, inc=1, device_id={"tp": place - 1}, device_id_type=MESH)
+
+    @pl.when(has_right)
+    def _():
+        pl.semaphore_signal(barrier, inc=1, device_id={"tp": place + 1}, device_id_type=MESH)
+
+    pl.semaphore_wait(barrier, ctx - 1 + has_left.astype(jnp.int32) + has_right.astype(jnp.int32))
+
+    def rightward(src, group, m):
+        return pltpu.make_async_remote_copy(
+            src_ref=src, dst_ref=right_buf.at[group, m], send_sem=right_send.at[group, m],
+            recv_sem=right_recv.at[group, m], device_id={"tp": place + 1}, device_id_type=MESH)
+
+    def leftward(src, group, m):
+        return pltpu.make_async_remote_copy(
+            src_ref=src, dst_ref=left_buf.at[group, m], send_sem=left_send.at[group, m],
+            recv_sem=left_recv.at[group, m], device_id={"tp": place - 1}, device_id_type=MESH)
+
+    def whole_tile(m):
+        return pl.ds(pl.multiple_of(m * rows, rows), rows)
+
+    def summed_tile(m):
+        return pl.ds(pl.multiple_of((tiles + m) * rows, rows), rows)
+
+    def share(m, dest):
+        cols = pl.ds(pl.multiple_of(dest * width, width), width)
+        return dot(gated_ref[summed_tile(m), :], w_ref[:, cols])
+
+    def first_step(m, _):
+        src = gated_ref.at[whole_tile(m)]
+
+        @pl.when(has_right)
+        def _():
+            rightward(src, 0, m).start()
+
+        @pl.when(has_left)
+        def _():
+            leftward(src, 0, m).start()
+        return 0
+
+    lax.fori_loop(0, tiles, first_step, 0)
+
+    def spread(d, k):
+        at = pl.ds(pl.multiple_of(me * piece, piece), piece)
+        return pltpu.make_async_remote_copy(
+            src_ref=slices[k], dst_ref=columns.at[k, at], send_sem=spread_send.at[d, k],
+            recv_sem=spread_recv.at[me, k], device_id={"ctx": lax.rem(me + d, ctx)}, device_id_type=MESH)
+
+    def gathered(d, k):
+        peer = lax.rem(me + d, ctx)
+        at = pl.ds(pl.multiple_of(peer * piece, piece), piece)
+        return pltpu.make_async_remote_copy(
+            src_ref=slices[k], dst_ref=columns.at[k, at], send_sem=spread_send.at[d, k],
+            recv_sem=spread_recv.at[peer, k], device_id={"ctx": peer}, device_id_type=MESH)
+
+    def kept(k):
+        at = pl.ds(pl.multiple_of(me * piece, piece), piece)
+        return pltpu.make_async_copy(slices[k], columns.at[k, at], own_sem.at[k])
+
+    def spread_step(d, _):
+        for k in range(tp - 1):
+            spread(d, k).start()
+        return 0
+
+    lax.fori_loop(1, ctx, spread_step, 0)
+    for k in range(tp - 1):
+        kept(k).start()
+    w_copy.wait()
+
+    def forward(group, m, steps_in, from_there, to_there, buf, copy, dest):
+        @pl.when(to_there & (group > steps_in))
+        def _():
+            part[...] = share(m, dest)
+
+        @pl.when(from_there)
+        def _():
+            copy(buf.at[group - 1, m], group - 1, m).wait_recv()
+
+        @pl.when(to_there & (group > steps_in) & from_there)
+        def _():
+            buf[group - 1, m] = (part[...] + buf[group - 1, m].astype(F32)).astype(BF16)
+
+        @pl.when(to_there & (group > steps_in) & jnp.logical_not(from_there))
+        def _():
+            buf[group - 1, m] = part[...].astype(BF16)
+
+        @pl.when(to_there)
+        def _():
+            copy(buf.at[group - 1, m], group, m).start()
+
+    def step(t, _):
+        group = t // tiles
+        m = t % tiles
+        forward(group, m, place, has_left, has_right, right_buf, rightward, tp + place - group)
+        forward(group, m, far, has_right, has_left, left_buf, leftward, group - far - 1)
+        return 0
+
+    lax.fori_loop(tiles, tp * tiles, step, 0)
+
+    def gathered_step(d, _):
+        for k in range(tp - 1):
+            gathered(d, k).wait_recv()
+        return 0
+
+    lax.fori_loop(1, ctx, gathered_step, 0)
+    for k in range(tp - 1):
+        kept(k).wait()
+
+    own_cols = pl.ds(pl.multiple_of(place * width, width), width)
+
+    def whole_step(m, _):
+        part[...] = dot(gated_ref[whole_tile(m), :], w_ref[:, own_cols])
+
+        def add_left(i, _):
+            part[...] += dot(right_buf[i, m], columns[i])
+            return 0
+
+        def add_right(i, _):
+            part[...] += dot(left_buf[i, m], columns[tp - 2 - i])
+            return 0
+
+        lax.fori_loop(0, place, add_left, 0)
+        lax.fori_loop(0, far, add_right, 0)
+        out_ref[whole_tile(m), :] = part[...].astype(BF16)
+        return 0
+
+    lax.fori_loop(0, tiles, whole_step, 0)
+
+    def summed_step(m, _):
+        part[...] = share(m, place)
+
+        @pl.when(has_left)
+        def _():
+            rightward(right_buf.at[tp - 1, m], tp - 1, m).wait_recv()
+            part[...] += right_buf[tp - 1, m].astype(F32)
+
+        @pl.when(has_right)
+        def _():
+            leftward(left_buf.at[tp - 1, m], tp - 1, m).wait_recv()
+            part[...] += left_buf[tp - 1, m].astype(F32)
+
+        out_ref[summed_tile(m), :] = part[...].astype(BF16)
+        return 0
+
+    lax.fori_loop(0, tiles, summed_step, 0)
+
+    def sent_step(t, _):
+        group = t // tiles
+        m = t % tiles
+
+        @pl.when(has_right)
+        def _():
+            rightward(right_buf.at[group, m], group, m).wait_send()
+
+        @pl.when(has_left)
+        def _():
+            leftward(left_buf.at[group, m], group, m).wait_send()
+        return 0
+
+    lax.fori_loop(0, tp * tiles, sent_step, 0)
+
+    def spread_done(d, _):
+        for k in range(tp - 1):
+            spread(d, k).wait_send()
+        return 0
+
+    lax.fori_loop(1, ctx, spread_done, 0)
+
+
+def project(gated, w_out, slices, ctx, tp, tiles):
+    block, width = gated.shape
+    rows = block // (2 * tiles)
+    vmem = pl.BlockSpec(memory_space=pltpu.VMEM)
+    return pl.pallas_call(
+        functools.partial(project_kernel, ctx, tp, tiles),
+        out_shape=jax.ShapeDtypeStruct((block, width), BF16),
+        in_specs=[vmem, pl.BlockSpec(memory_space=pl.ANY)] + [vmem] * (tp - 1),
+        out_specs=vmem,
+        scratch_shapes=[
+            pltpu.VMEM(w_out.shape, BF16),
+            pltpu.VMEM((tp - 1, w_out.shape[0], width), BF16),
+            pltpu.VMEM((tp, tiles, rows, width), BF16),
+            pltpu.VMEM((tp, tiles, rows, width), BF16),
+            pltpu.VMEM((rows, width), F32),
+            pltpu.SemaphoreType.DMA,
+            pltpu.SemaphoreType.DMA((tp - 1,)),
+            pltpu.SemaphoreType.DMA((ctx, tp - 1)),
+            pltpu.SemaphoreType.DMA((ctx, tp - 1)),
+            pltpu.SemaphoreType.DMA((tp, tiles)),
+            pltpu.SemaphoreType.DMA((tp, tiles)),
+            pltpu.SemaphoreType.DMA((tp, tiles)),
+            pltpu.SemaphoreType.DMA((tp, tiles)),
+        ],
+        compiler_params=pltpu.CompilerParams(
+            collective_id=1, has_side_effects=True, vmem_limit_bytes=48 * 2**20),
+        cost_estimate=pl.CostEstimate(
+            flops=2 * block * width * width * tp, bytes_accessed=8 * block * width, transcendentals=0),
+        name="project",
+    )(gated, w_out, *slices)
+
+
 def on_device(ctx, tp, query, keys, values, residues, rates, w_out):
     width = keys.shape[1]
     groups = width // SHARE
     place = lax.axis_index("tp")
+    piece = w_out.shape[0] // ctx
+    first = lax.axis_index("ctx") * piece
+    slices = []
+    for k in range(1, tp):
+        to = lax.rem(place + k, tp)
+        mine = lax.dynamic_slice(w_out, (first, to * width), (piece, width))
+        slices.append(lax.ppermute(mine, "tp", [(i, (i + k) % tp) for i in range(tp)]))
     rates = lax.dynamic_slice_in_dim(rates, place * groups, groups, 0)
     residues = lax.dynamic_slice_in_dim(residues, place * groups, groups, 0)
     gain = residues * jnp.sqrt(2.0 * rates)
     gated = gated_conv(query, keys, values, rates, gain, ctx)
-    mixed = dot(gated, w_out).astype(BF16)
-    return lax.psum_scatter(mixed, "tp", scatter_dimension=1, tiled=True)
+    return project(gated, w_out, slices, ctx, tp, 4)
 
 
 def solution(mesh):

time: 195 us -> 130 us (0.67)
  the two profiles are of different devices: /device:TPU:14 before, /device:TPU:0 now
where the time goes in v1:
time: 130 us
  Pallas kernels  113 us (87%)
  local copies, waits for them, and re-layouts  9.6 us (7%)
  starting transfers between devices  6.06 us (5%)
    pallas_call x1, Pallas kernels, project(): pl.pallas_call(functools.partial(project_kernel, ctx, tp, tiles), out_sha...  97.4 us
    pallas_call x1, Pallas kernels, gated_conv(): pl.pallas_call(functools.partial(conv_kernel, ctx, state, chunk), out_sha...  15.9 us
    ppermute x3, starting transfers between devices, on_device(): lax.ppermute(mine, 'tp', [(i, (i + k) % tp) for i in range(tp)])  6.06 us
    unnamed x7, local copies, waits for them, and re-layouts  4.5 us
  transfers between devices with their start and end apart: 3, of which 0 were waited for; matrix products, arithmetic and copies ran while one was open for 3% of the time, Pallas kernels for 12%

profile of v1, /device:TPU:0, one launch (start us, length us, event | category | flops | bytes accessed | tf_op | source)
XLA Modules:
  0.0 130.0 jit_solution(9250084976880417241)
XLA Ops:
  0.0 0.0 copy-start
  0.0 2.2 %fusion.1 = (bf16[128,1024]{1,0:T(8,128)(2,1)}, bf16[128,1024]{1,0:T(8,128)(2,1)}, bf16[128,1024]{1,0:T(8,128)(2,1)}) fusion(bf16[1024,4096]{1,0:T(8,128)(2,1)} %w_hbm.1, s32[]{:T(128)S(6)} %select_n.41, s32[]{:T(128)S(6)} %select_n.44, s32[]{:T(128)S(6)} %select_n.43, s32[]{:T(128)S(6)} %select_n.42), kind=kLoop, calls=%fused_computation.9 | loop fusion | bytes 1572880 | tf_op jit(solution)/shard_map/dynamic_slice | solution.py:412
  2.2 5.0 %collective-permute-start.2 = (bf16[128,1024]{1,0:T(8,128)(2,1)}, bf16[128,1024]{1,0:T(8,128)(2,1)S(1)}, u32[]{:S(2)}, u32[]{:S(2)}) collective-permute-start(bf16[128,1024]{1,0:T(8,128)(2,1)} %get-tuple-element.7), channel_id=1, source_target_pairs={{0,3},{1,0},{2,1},{3,2},{4,7},{5,4},{6,5},{7,6},{8,11},{9,8},{10,9... | collective-permute-start | bytes 786440 | tf_op jit(solution)/shard_map/ppermute | solution.py:413
  7.2 0.0 collective-permute-start.1
  7.2 1.0 collective-permute-start
  8.3 0.1 compare_convert_fusion.gmask_ref
  8.3 0.8 sqrt_multiply_fusion
  9.1 0.1 copy.10
  9.2 0.1 reshape.86.rrow_ref
  9.3 0.3 reshape.90.rcol_ref
  9.6 0.1 copy.11
  9.7 0.1 reshape.87.grow_ref
  9.8 1.0 broadcast_in_dim.2
  10.8 1.3 %reshape.89.rlane_ref = f32[16,1024]{1,0:T(8,128)S(1)} reshape(f32[16,64,16]{2,1,0:T(8,128)} %broadcast_in_dim.2) | data formatting | bytes 131072 | tf_op jit(solution)/shard_map/reshape | solution.py:173
  12.1 0.0 copy-done
  12.1 0.0 copy-start.1
  12.1 1.6 %copy-done.1 = bf16[1024,1024]{1,0:T(8,128)(2,1)S(1)} copy-done((bf16[1024,1024]{1,0:T(8,128)(2,1)S(1)}, bf16[1024,1024]{1,0:T(8,128)(2,1)}, u32[]{:S(2)}) %copy-start.1) | copy-done | bytes 2097176
  13.7 0.0 copy-start.2
  13.7 1.6 %copy-done.2 = bf16[1024,1024]{1,0:T(8,128)(2,1)S(1)} copy-done((bf16[1024,1024]{1,0:T(8,128)(2,1)S(1)}, bf16[1024,1024]{1,0:T(8,128)(2,1)}, u32[]{:S(2)}) %copy-start.2) | copy-done | bytes 2097176
  15.3 15.9 %gated_conv.1.gated_ref = bf16[1024,1024]{1,0:T(8,128)(2,1)S(1)} custom-call(bf16[1024,1024]{1,0:T(8,128)(2,1)S(1)} %copy-done, bf16[1024,1024]{1,0:T(8,128)(2,1)S(1)} %copy-done.1, bf16[1024,1024]{1,0:T(8,128)(2,1)S(1)} %copy-done.2, f32[8,128]{1,0:T(8,128)S(1)} %reshape.86.rrow_ref, f32[8,128]{1,0:T(8,128)S(1)} %reshape.87.grow_ref, ...), custom_call_target="tpu_custom_call" | custom-call | flops 5368709120 | bytes 8388608 | tf_op jit(solution)/shard_map/gated_conv/pallas_call | solution.py:151
  31.2 0.0 collective-permute-done.2.rest_2_
  31.2 0.0 collective-permute-done.1.rest_1_
  31.2 0.0 collective-permute-done.rest_0_
  31.2 97.4 %project.1 = bf16[1024,1024]{1,0:T(8,128)(2,1)S(1)} custom-call(bf16[1024,1024]{1,0:T(8,128)(2,1)S(1)} %gated_conv.1.gated_ref, bf16[1024,4096]{1,0:T(8,128)(2,1)} %w_hbm.1, bf16[128,1024]{1,0:T(8,128)(2,1)S(1)} %collective-permute-done.rest_0_, bf16[128,1024]{1,0:T(8,128)(2,1)S(1)} %collective-permute-done.1.rest_1_, ...), custom_call_target="tpu_custom_call" | custom-call | flops 8589934592 | bytes 8388608 | tf_op jit(solution)/shard_map/project/pallas_call | solution.py:375
  128.6 1.3 %copy.15 = bf16[1024,1024]{1,0:T(8,128)(2,1)} copy(bf16[1024,1024]{1,0:T(8,128)(2,1)S(1)} %project.1) | data formatting | bytes 4194304
  (2 shorter events, 0.0 us)
Async XLA Ops:
  0.0 12.1 %copy-start = (bf16[1024,1024]{1,0:T(8,128)(2,1)S(1)}, bf16[1024,1024]{1,0:T(8,128)(2,1)}, u32[]{:S(2)}) copy-start(bf16[1024,1024]{1,0:T(8,128)(2,1)} %q_ref.1) | copy-start | bytes 6291460
  2.2 29.0 %collective-permute-start.2 = (bf16[128,1024]{1,0:T(8,128)(2,1)}, bf16[128,1024]{1,0:T(8,128)(2,1)S(1)}, u32[]{:S(2)}, u32[]{:S(2)}) collective-permute-start(bf16[128,1024]{1,0:T(8,128)(2,1)} %get-tuple-element.7), channel_id=1, source_target_pairs={{0,3},{1,0},{2,1},{3,2},{4,7},{5,4},{6,5},{7,6},{8,11},{9,8},{10,9... | collective-permute-start | bytes 786440 | tf_op jit(solution)/shard_map/ppermute | solution.py:413
  7.2 24.0 %collective-permute-start.1 = (bf16[128,1024]{1,0:T(8,128)(2,1)}, bf16[128,1024]{1,0:T(8,128)(2,1)S(1)}, u32[]{:S(2)}, u32[]{:S(2)}) collective-permute-start(bf16[128,1024]{1,0:T(8,128)(2,1)} %get-tuple-element.8), channel_id=1, source_target_pairs={{0,2},{1,3},{2,0},{3,1},{4,6},{5,7},{6,4},{7,5},{8,10},{9,11},{10,... | collective-permute-start | bytes 786440 | tf_op jit(solution)/shard_map/ppermute | solution.py:413
  7.2 24.0 %collective-permute-start = (bf16[128,1024]{1,0:T(8,128)(2,1)}, bf16[128,1024]{1,0:T(8,128)(2,1)S(1)}, u32[]{:S(2)}, u32[]{:S(2)}) collective-permute-start(bf16[128,1024]{1,0:T(8,128)(2,1)} %get-tuple-element.9), channel_id=1, source_target_pairs={{0,1},{1,2},{2,3},{3,0},{4,5},{5,6},{6,7},{7,4},{8,9},{9,10},{10,1... | collective-permute-start | bytes 786440 | tf_op jit(solution)/shard_map/ppermute | solution.py:413
  12.1 1.6 %copy-start.1 = (bf16[1024,1024]{1,0:T(8,128)(2,1)S(1)}, bf16[1024,1024]{1,0:T(8,128)(2,1)}, u32[]{:S(2)}) copy-start(bf16[1024,1024]{1,0:T(8,128)(2,1)} %k_ref.1) | copy-start | bytes 6291460
  13.7 1.6 %copy-start.2 = (bf16[1024,1024]{1,0:T(8,128)(2,1)S(1)}, bf16[1024,1024]{1,0:T(8,128)(2,1)}, u32[]{:S(2)}) copy-start(bf16[1024,1024]{1,0:T(8,128)(2,1)} %v_ref.1) | copy-start | bytes 6291460

commit v2 on v0

v2 whole, which is shorter than its diff:
```python
import functools
import math

import jax
import jax.numpy as jnp
import numpy as np
from jax import lax
from jax.experimental import pallas as pl
from jax.experimental.pallas import tpu as pltpu
from jax.sharding import PartitionSpec as P

SHARE = 16
LANES = 128
MESH = pl.DeviceIdType.MESH
F32 = jnp.float32
BF16 = jnp.bfloat16


def split(x):
    upper = x.astype(BF16)
    return upper, (x - upper.astype(F32)).astype(BF16)


def dot(a, b):
    return jnp.dot(a, b, preferred_element_type=F32)


def layer_kernel(ctx, tp, tiles, state, chunk, q_hbm, k_hbm, v_hbm, w_hbm, rates_ref, residues_ref, gmask_ref,
                 smask_ref, out_ref, q_ref, k_ref, v_ref, w_ref, gated, states, own, before, inside, wide, taps,
                 carry, extra, right_buf, left_buf, stage, part, load_sem, state_send, state_recv, hop_send,
                 hop_recv, spread_send, spread_recv, right_send, right_recv, left_send, left_recv):
    block, width = out_ref.shape
    chunks = block // chunk
    half = chunks // 2
    lane_blocks = width // LANES
    groups = LANES // SHARE
    modes = groups * state
    rows = block // (2 * tiles)
    piece = width // ctx
    inner = tp - 2
    me = lax.axis_index("ctx")
    place = lax.axis_index("tp")
    far = tp - 1 - place
    has_left = place > 0
    has_right = far > 0
    is_helper = (place == 1) | (far == 1)

    loads = [pltpu.make_async_copy(src, dst, load_sem.at[i]) for i, (src, dst) in enumerate(
        [(k_hbm, k_ref), (v_hbm, v_ref), (q_hbm, q_ref), (w_hbm, w_ref)])]
    for load in loads:
        load.start()

    barrier = pltpu.get_barrier_semaphore()

    def greet(d, _):
        pl.semaphore_signal(barrier, inc=1, device_id={"ctx": lax.rem(me + d, ctx)}, device_id_type=MESH)
        return 0

    lax.fori_loop(1, ctx, greet, 0)

    @pl.when(has_left)
    def _():
        pl.semaphore_signal(barrier, inc=1, device_id={"tp": place - 1}, device_id_type=MESH)

    @pl.when(has_right)
    def _():
        pl.semaphore_signal(barrier, inc=1, device_id={"tp": place + 1}, device_id_type=MESH)

    pl.semaphore_wait(barrier, ctx - 1 + has_left.astype(jnp.int32) + has_right.astype(jnp.int32))

    def column_block(order, from_left):
        return jnp.where(from_left, tp - 2 - order, order)

    def piece_rows(j):
        return pl.ds(pl.multiple_of(j * piece, piece), piece)

    def hop(order, to_right):
        e = column_block(order, to_right)
        cols = pl.ds(pl.multiple_of(jnp.where(to_right, e + 1, e) * width, width), width)
        return pltpu.make_async_remote_copy(
            src_ref=w_hbm.at[piece_rows(me), cols], dst_ref=extra.at[e, piece_rows(me)],
            send_sem=hop_send.at[e], recv_sem=hop_recv.at[e],
            device_id={"tp": jnp.where(to_right, place + 1, place - 1)}, device_id_type=MESH)

    def hop_step(order, _):
        hop(order, place == 0).start()
        return 0

    @pl.when((place == 0) | (far == 0))
    def _():
        lax.fori_loop(0, tp - 1, hop_step, 0)

    def spread(order, d):
        e = column_block(order, place == 1)
        return pltpu.make_async_remote_copy(
            src_ref=extra.at[e, piece_rows(me)], dst_ref=extra.at[e, piece_rows(me)],
            send_sem=spread_send.at[e, d], recv_sem=spread_recv.at[e, me],
            device_id={"ctx": lax.rem(me + d, ctx)}, device_id_type=MESH)

    def gathered(order, d):
        e = column_block(order, place == 1)
        peer = lax.rem(me + d, ctx)
        return pltpu.make_async_remote_copy(
            src_ref=extra.at[e, piece_rows(peer)], dst_ref=extra.at[e, piece_rows(peer)],
            send_sem=spread_send.at[e, d], recv_sem=spread_recv.at[e, peer],
            device_id={"ctx": peer}, device_id_type=MESH)

    def spread_block(order):
        e = column_block(order, place == 1)
        pltpu.make_async_remote_copy(
            src_ref=w_hbm.at[piece_rows(me), pl.ds(0, width)], dst_ref=extra.at[e, piece_rows(me)],
            send_sem=hop_send.at[e], recv_sem=hop_recv.at[e],
            device_id={"tp": jnp.where(place == 1, place - 1, place + 1)}, device_id_type=MESH).wait_recv()
        lax.fori_loop(1, ctx, lambda d, _: (spread(order, d).start(), 0)[1], 0)

    def await_block(order):
        lax.fori_loop(1, ctx, lambda d, _: (gathered(order, d).wait_recv(), 0)[1], 0)

    def product(k, lanes):
        at = pl.ds(k * chunk, chunk)
        return (k_ref[at, lanes].astype(F32) * v_ref[at, lanes].astype(F32)).astype(BF16)

    def lanes_of(b):
        return pl.ds(pl.multiple_of(b * LANES, LANES), LANES)

    def rate_row(b):
        return rates_ref[pl.ds(place * lane_blocks + b, 1), :]

    def gain_row(b):
        return residues_ref[pl.ds(place * lane_blocks + b, 1), :] * jnp.sqrt(2.0 * rate_row(b))

    def rate_columns(b):
        return jnp.broadcast_to(rate_row(b), (LANES, modes)).T

    def rate_lanes(b):
        return (rate_columns(b) * gmask_ref[...]).reshape(groups, state, LANES).sum(0)

    def state_step(b, _):
        lanes = lanes_of(b)
        tau = lax.broadcasted_iota(jnp.int32, (modes, chunk), 1).astype(F32)
        upper, lower = split(jnp.exp(-rate_columns(b) * (chunk - 1.0 - tau)))
        decay = jnp.exp(-rate_lanes(b) * float(chunk))
        gmask = gmask_ref[...]
        total = jnp.zeros((state, LANES), F32)
        for k in range(chunks):
            x = product(k, lanes)
            fresh = (dot(upper, x) + dot(lower, x)) * gmask
            before[k, :, lanes] = total
            total = total * decay + fresh.reshape(groups, state, LANES).sum(0)
        own[:, lanes] = total
        return 0

    loads[0].wait()
    loads[1].wait()
    lax.fori_loop(0, lane_blocks, state_step, 0)

    def to_peer(d):
        return pltpu.make_async_remote_copy(
            src_ref=own, dst_ref=states.at[me], send_sem=state_send.at[d], recv_sem=state_recv.at[me],
            device_id={"ctx": lax.rem(me + d, ctx)}, device_id_type=MESH)

    def from_peer(j):
        return pltpu.make_async_remote_copy(
            src_ref=own, dst_ref=states.at[j], send_sem=state_send.at[0], recv_sem=state_recv.at[j],
            device_id={"ctx": j}, device_id_type=MESH)

    lax.fori_loop(1, ctx - me, lambda d, _: (to_peer(d).start(), 0)[1], 0)

    def taps_step(b):
        row = lax.broadcasted_iota(jnp.int32, (chunk, modes), 0).astype(F32)
        col = lax.broadcasted_iota(jnp.int32, (modes, chunk), 1).astype(F32)
        middle = chunk / 2.0
        falling = gain_row(b) * jnp.exp(-rate_row(b) * (row - middle))
        b_hi, b_lo = split(jnp.exp(rate_columns(b) * (col - middle)))
        causal = lax.broadcasted_iota(jnp.int32, (chunk, chunk), 0) >= lax.broadcasted_iota(
            jnp.int32, (chunk, chunk), 1)
        for g in range(groups):
            a_hi, a_lo = split(falling * smask_ref[g:g + 1, :])
            tap = dot(a_hi, b_hi) + dot(a_lo, b_hi) + dot(a_hi, b_lo)
            taps[b, :, g * chunk:(g + 1) * chunk] = jnp.where(causal, tap, 0.0).astype(BF16)

    def inside_step(b, first):
        lanes = lanes_of(b)
        xs = [product(first + k, lanes) for k in range(half)]
        for g in range(groups):
            only = gmask_ref[g * state:g * state + 1, :].astype(BF16)
            for k in range(half):
                wide[g * chunk:(g + 1) * chunk, k * LANES:(k + 1) * LANES] = xs[k] * only
        inside[b] = dot(taps[b], wide[...])

    def carry_step(b, first):
        lanes = lanes_of(b)
        rlane = rate_lanes(b)
        along = jnp.exp(-rlane * float(block))
        decay = jnp.exp(-rlane * float(chunk))
        reached = lax.fori_loop(
            0, me, lambda j, r: r * along + states[j, :, lanes], jnp.zeros((state, LANES), F32))
        reached = reached * jnp.exp(-rlane * float(chunk * first))
        gmask = gmask_ref[...]
        for k in range(half):
            entering = before[first + k, :, lanes] + reached
            reached = reached * decay
            hi, lo = split(jnp.concatenate([entering] * groups, axis=0) * gmask)
            at = slice(k * LANES, (k + 1) * LANES)
            carry[0:modes, at] = hi
            carry[modes:2 * modes, at] = hi
            carry[2 * modes:3 * modes, at] = lo
        row = lax.broadcasted_iota(jnp.int32, (chunk, modes), 0).astype(F32)
        hi, lo = split(gain_row(b) * jnp.exp(-rate_row(b) * (row + 1.0)))
        full = inside[b] + dot(jnp.concatenate([hi, lo, hi], axis=1), carry[...])
        for k in range(half):
            at = pl.ds((first + k) * chunk, chunk)
            convolved = full[:, k * LANES:(k + 1) * LANES].astype(BF16)
            gated[at, lanes] = (q_ref[at, lanes].astype(F32) * convolved.astype(F32)).astype(BF16)

    def early_inside(b, _):
        taps_step(b)
        inside_step(b, 0)
        return 0

    def early_carry(b, _):
        carry_step(b, 0)
        return 0

    def late_step(b, _):
        inside_step(b, half)
        carry_step(b, half)
        return 0

    lax.fori_loop(0, lane_blocks, early_inside, 0)
    lax.fori_loop(0, me, lambda j, _: (from_peer(j).wait_recv(), 0)[1], 0)
    loads[2].wait()
    lax.fori_loop(0, lane_blocks, early_carry, 0)
    loads[3].wait()

    def early_tile(m):
        return pl.ds(pl.multiple_of(m * rows, rows), rows)

    def late_tile(m):
        return pl.ds(pl.multiple_of((tiles + m) * rows, rows), rows)

    def share(tile, dest):
        cols = pl.ds(pl.multiple_of(dest * width, width), width)
        return dot(gated[tile, :], w_ref[:, cols])

    def rightward(src, h, i, m):
        return pltpu.make_async_remote_copy(
            src_ref=src, dst_ref=right_buf.at[h, i, m], send_sem=right_send.at[h, i, m],
            recv_sem=right_recv.at[h, i, m], device_id={"tp": place + 1}, device_id_type=MESH)

    def leftward(src, h, i, m):
        return pltpu.make_async_remote_copy(
            src_ref=src, dst_ref=left_buf.at[h, i, m], send_sem=left_send.at[h, i, m],
            recv_sem=left_recv.at[h, i, m], device_id={"tp": place - 1}, device_id_type=MESH)

    flows = ((place, rightward, right_buf, lambda d: d), (far, leftward, left_buf, lambda d: tp - 1 - d))

    def sums_step(flow, h, i, m, tile, go):
        role, copy, buf, physical = flow
        came = i - (role >= 2).astype(jnp.int32)
        dest = tp - 1 - i + jnp.maximum(role - 1, 0)

        @pl.when(go)
        def _():
            part[...] = share(tile, physical(dest))

        @pl.when(go & (role > 0))
        def _():
            copy(buf.at[h, came, m], h, came, m).wait_recv()
            buf[h, came, m] = (part[...] + buf[h, came, m].astype(F32)).astype(BF16)

        @pl.when(go & (role == 0))
        def _():
            buf[h, came, m] = part[...].astype(BF16)

        @pl.when(go)
        def _():
            copy(buf.at[h, came, m], h, i, m).start()

    def early_step(t, _):
        i = t // tiles
        m = t % tiles
        for flow in flows:
            sums_step(flow, 0, i, m, early_tile(m), i >= flow[0] - 1)

        @pl.when(is_helper & (t < tp - 1))
        def _():
            spread_block(t)

        @pl.when(t < lane_blocks)
        def _():
            late_step(t, 0)
        return 0

    steps = inner * tiles
    lax.fori_loop(0, steps, early_step, 0)
    lax.fori_loop(steps, max(steps, lane_blocks), late_step, 0)

    def end_step(flow, i, m):
        role, copy, buf, physical = flow

        @pl.when((role == 0) & (i == 0))
        def _():
            copy(gated.at[late_tile(m)], 1, 0, m).start()

        @pl.when((role == 0) & (i == 1))
        def _():
            buf[1, 1, m] = share(early_tile(m), physical(1)).astype(BF16)
            copy(buf.at[1, 1, m], 1, 1, m).start()

    def helper_step(flow, i, m):
        role, copy, buf, physical = flow

        @pl.when(role == 1)
        def _():
            part[...] = share(late_tile(m), physical(tp - 1 - i))

            @pl.when(i == 0)
            def _():
                copy(buf.at[1, 0, m], 1, 0, m).wait_recv()

            @pl.when(m == 0)
            def _():
                await_block(i)

            stage[i, m] = (part[...] + dot(buf[1, 0, m], extra[column_block(i, place == 1)])).astype(BF16)
            copy(stage.at[i, m], 1, i, m).start()

    def late_sums(t, _):
        i = t // tiles
        m = t % tiles
        for flow in flows:
            end_step(flow, i, m)
            helper_step(flow, i, m)
            sums_step(flow, 1, i, m, late_tile(m), (flow[0] >= 2) & (i >= flow[0] - 1))
        return 0

    lax.fori_loop(0, steps, late_sums, 0)

    @pl.when(is_helper)
    def _():
        await_block(tp - 2)

    def last_step(m, _):
        part[...] = share(late_tile(m), place)
        for role, copy, buf, _physical in flows:
            @pl.when(role == 1)
            def _():
                part[...] += dot(buf[1, 0, m], extra[column_block(tp - 2, place == 1)])

            @pl.when(role >= 2)
            def _():
                copy(buf.at[1, inner - 1, m], 1, inner - 1, m).wait_recv()
                part[...] += buf[1, inner - 1, m].astype(F32)

        out_ref[late_tile(m), :] = part[...].astype(BF16)
        part[...] = share(early_tile(m), place)
        for role, copy, buf, _physical in flows:
            @pl.when(role == 1)
            def _():
                copy(buf.at[1, 1, m], 1, 1, m).wait_recv()
                part[...] += buf[1, 1, m].astype(F32)

            @pl.when(role >= 2)
            def _():
                copy(buf.at[0, inner - 1, m], 0, inner - 1, m).wait_recv()
                part[...] += buf[0, inner - 1, m].astype(F32)

        out_ref[early_tile(m), :] = part[...].astype(BF16)
        return 0

    lax.fori_loop(0, tiles, last_step, 0)

    def sent_step(t, _):
        i = t // tiles
        m = t % tiles
        for role, copy, buf, _physical in flows:
            for h in range(2):
                early_end = (role == 0) if h == 0 else (role == 0) & (i < 2)

                @pl.when(early_end | ((role > 0) & (i >= role - 1)))
                def _():
                    copy(buf.at[h, i, m], h, i, m).wait_send()
        return 0

    lax.fori_loop(0, steps, sent_step, 0)
    lax.fori_loop(1, ctx - me, lambda d, _: (to_peer(d).wait_send(), 0)[1], 0)

    @pl.when((place == 0) | (far == 0))
    def _():
        lax.fori_loop(0, tp - 1, lambda o, _: (hop(o, place == 0).wait_send(), 0)[1], 0)

    @pl.when(is_helper)
    def _():
        for order in range(tp - 1):
            lax.fori_loop(1, ctx, lambda d, _: (spread(order, d).wait_send(), 0)[1], 0)


def on_device(ctx, tp, query, keys, values, residues, rates, w_out):
    block, width = keys.shape
    state = rates.shape[1]
    chunk = math.gcd(block, LANES)
    chunks = block // chunk
    half = chunks // 2
    groups = LANES // SHARE
    modes = groups * state
    lane_blocks = width // LANES
    tiles = 4
    inner = tp - 2
    rows = block // (2 * tiles)
    at_row = np.arange(modes) // state
    gmask = jnp.asarray((at_row[:, None] == np.arange(LANES)[None, :] // SHARE).astype(np.float32))
    smask = jnp.asarray((np.arange(groups)[:, None] == at_row[None, :]).astype(np.float32))
    vmem = pl.BlockSpec(memory_space=pltpu.VMEM)
    hbm = pl.BlockSpec(memory_space=pl.ANY)
    dma = pltpu.SemaphoreType.DMA
    return pl.pallas_call(
        functools.partial(layer_kernel, ctx, tp, tiles, state, chunk),
        out_shape=jax.ShapeDtypeStruct((block, width), BF16),
        in_specs=[hbm] * 4 + [vmem] * 4,
        out_specs=vmem,
        scratch_shapes=[
            pltpu.VMEM((block, width), BF16),
            pltpu.VMEM((block, width), BF16),
            pltpu.VMEM((block, width), BF16),
            pltpu.VMEM(w_out.shape, BF16),
            pltpu.VMEM((block, width), BF16),
            pltpu.VMEM((ctx, state, width), F32),
            pltpu.VMEM((state, width), F32),
            pltpu.VMEM((chunks, state, width), F32),
            pltpu.VMEM((lane_blocks, chunk, half * LANES), F32),
            pltpu.VMEM((groups * chunk, half * LANES), BF16),
            pltpu.VMEM((lane_blocks, chunk, groups * chunk), BF16),
            pltpu.VMEM((3 * modes, half * LANES), BF16),
            pltpu.VMEM((tp - 1, width, width), BF16),
            pltpu.VMEM((2, inner, tiles, rows, width), BF16),
            pltpu.VMEM((2, inner, tiles, rows, width), BF16),
            pltpu.VMEM((inner, tiles, rows, width), BF16),
            pltpu.VMEM((rows, width), F32),
            dma((4,)),
            dma((ctx,)),
            dma((ctx,)),
            dma((tp - 1,)),
            dma((tp - 1,)),
            dma((tp - 1, ctx)),
            dma((tp - 1, ctx)),
            dma((2, inner, tiles)),
            dma((2, inner, tiles)),
            dma((2, inner, tiles)),
            dma((2, inner, tiles)),
        ],
        compiler_params=pltpu.CompilerParams(
            collective_id=0, has_side_effects=True, vmem_limit_bytes=56 * 2**20),
        cost_estimate=pl.CostEstimate(
            flops=4 * block * width * width * tp, bytes_accessed=24 * block * width, transcendentals=0),
        name="hyena_layer",
    )(query, keys, values, w_out, rates.reshape(-1, modes), residues.reshape(-1, modes), gmask, smask)


def solution(mesh):
    in_specs = (P("ctx", "tp"), P("ctx", "tp"), P("ctx", "tp"), P(), P(), P("tp", None))
    return jax.shard_map(
        functools.partial(on_device, mesh.shape["ctx"], mesh.shape["tp"]),
        mesh=mesh, in_specs=in_specs, out_specs=P("ctx", "tp"), check_vma=False)
```

time: 195 us -> 131 us (0.67)
  waiting for transfers between devices: 145 us -> 0 us
  Pallas kernels: 16 us -> 123 us
  between operations: 13.4 us -> 0.01 us
  matrix products: 10.8 us -> 0 us
    reduce_scatter x1 -> x0, waiting for transfers between devices: 145 us -> none  [on_device(): return lax.psum_scatter(mixed, 'tp', scatter_dimension=1, tiled=True)]
    pallas_call x1, Pallas kernels: 16 us -> 123 us  [on_device(): pl.pallas_call(functools.partial(layer_kernel, ctx, tp, tiles, state, chu...]
    dot_general x1 -> x0, matrix products: 10.8 us -> none  [dot(): return jnp.dot(a, b, preferred_element_type=F32)]
    unnamed x8 -> x3, local copies, waits for them, and re-layouts: 4.77 us -> 4.71 us
  transfers between devices with their start and end apart: 1 -> 0, of which waited for: 1 -> 0; matrix products, arithmetic and copies ran while one was open for 0% -> 0% of each run, Pallas kernels for 0% -> 0%
where the time goes in v2:
time: 131 us; the launch traced here: 129 us
  Pallas kernels  123 us (94%)
  local copies, waits for them, and re-layouts  6.11 us (5%)
    pallas_call x1, Pallas kernels, on_device(): pl.pallas_call(functools.partial(layer_kernel, ctx, tp, tiles, state, chu...  123 us
    unnamed x3, local copies, waits for them, and re-layouts  4.71 us

profile of v2, /device:TPU:14, one launch (start us, length us, event | category | flops | bytes accessed | tf_op | source)
XLA Modules:
  0.0 128.9 jit_solution(12589561428153185797)
XLA Ops:
  0.0 0.8 copy.12
  0.8 0.7 reshape.7.residues_ref
  1.5 0.8 copy.11
  2.3 0.7 reshape.6.rates_ref
  3.0 122.7 %hyena_layer.1 = bf16[1024,1024]{1,0:T(8,128)(2,1)} custom-call(bf16[1024,1024]{1,0:T(8,128)(2,1)} %q_hbm.1, bf16[1024,1024]{1,0:T(8,128)(2,1)} %k_hbm.1, bf16[1024,1024]{1,0:T(8,128)(2,1)} %v_hbm.1, bf16[1024,4096]{1,0:T(8,128)(2,1)} %w_hbm.1, f32[32,128]{1,0:T(8,128)} %reshape.6.rates_ref, f32[32,128]{1,0:T(8,128)} %reshape.7.residues_ref, ...), custom_call_target="tpu_custom_call" | custom-call | flops 17179869184 | bytes 25165824 | tf_op jit(solution)/shard_map/hyena_layer/pallas_call | solution.py:417
  125.8 3.1 %copy.14 = bf16[1024,1024]{1,0:T(8,128)(2,1)} copy(bf16[1024,1024]{1,0:T(8,128)(2,1)} %hyena_layer.1) | data formatting | bytes 4194304

commit v3 on v2

--- a/solution.py
+++ b/solution.py
@@ -26,8 +26,8 @@
 
 
 def layer_kernel(ctx, tp, tiles, state, chunk, q_hbm, k_hbm, v_hbm, w_hbm, rates_ref, residues_ref, gmask_ref,
-                 smask_ref, out_ref, q_ref, k_ref, v_ref, w_ref, gated, states, own, before, inside, wide, taps,
-                 carry, extra, right_buf, left_buf, stage, part, load_sem, state_send, state_recv, hop_send,
+                 smask_ref, out_ref, q_ref, k_ref, v_ref, w_ref, columns, rate_rows, gain_rows, gated, states, own, before,
+                 inside, wide, taps, carry, extra, right_buf, left_buf, stage, part, load_sem, state_send, state_recv, hop_send,
                  hop_recv, spread_send, spread_recv, right_send, right_recv, left_send, left_recv):
     block, width = out_ref.shape
     chunks = block // chunk
@@ -47,8 +47,8 @@
 
     loads = [pltpu.make_async_copy(src, dst, load_sem.at[i]) for i, (src, dst) in enumerate(
         [(k_hbm, k_ref), (v_hbm, v_ref), (q_hbm, q_ref), (w_hbm, w_ref)])]
-    for load in loads:
-        load.start()
+    loads[0].start()
+    loads[1].start()
 
     barrier = pltpu.get_barrier_semaphore()
 
@@ -90,20 +90,24 @@
     def _():
         lax.fori_loop(0, tp - 1, hop_step, 0)
 
-    def spread(order, d):
+    chips = ctx // 2
+    sibling = me + 1 - 2 * lax.rem(me, 2)
+
+    def chip_peer(d):
+        return lax.rem(me + 2 * d, ctx)
+
+    def carried(order, j, send, peer):
         e = column_block(order, place == 1)
         return pltpu.make_async_remote_copy(
-            src_ref=extra.at[e, piece_rows(me)], dst_ref=extra.at[e, piece_rows(me)],
-            send_sem=spread_send.at[e, d], recv_sem=spread_recv.at[e, me],
-            device_id={"ctx": lax.rem(me + d, ctx)}, device_id_type=MESH)
-
-    def gathered(order, d):
-        e = column_block(order, place == 1)
-        peer = lax.rem(me + d, ctx)
-        return pltpu.make_async_remote_copy(
-            src_ref=extra.at[e, piece_rows(peer)], dst_ref=extra.at[e, piece_rows(peer)],
-            send_sem=spread_send.at[e, d], recv_sem=spread_recv.at[e, peer],
+            src_ref=extra.at[e, piece_rows(j)], dst_ref=extra.at[e, piece_rows(j)],
+            send_sem=spread_send.at[e, send], recv_sem=spread_recv.at[e, j],
             device_id={"ctx": peer}, device_id_type=MESH)
+
+    def across(order, d):
+        return carried(order, me, d, chip_peer(d))
+
+    def beside(order, d):
+        return carried(order, chip_peer(d), chips + d, sibling)
 
     def spread_block(order):
         e = column_block(order, place == 1)
@@ -111,10 +115,24 @@
             src_ref=w_hbm.at[piece_rows(me), pl.ds(0, width)], dst_ref=extra.at[e, piece_rows(me)],
             send_sem=hop_send.at[e], recv_sem=hop_recv.at[e],
             device_id={"tp": jnp.where(place == 1, place - 1, place + 1)}, device_id_type=MESH).wait_recv()
-        lax.fori_loop(1, ctx, lambda d, _: (spread(order, d).start(), 0)[1], 0)
+        lax.fori_loop(1, chips, lambda d, _: (across(order, d).start(), 0)[1], 0)
+        beside(order, 0).start()
+
+    def relay_block(order):
+        def relay(d, _):
+            carried(order, chip_peer(d), d, chip_peer(d)).wait_recv()
+            beside(order, d).start()
+            return 0
+
+        lax.fori_loop(1, chips, relay, 0)
 
     def await_block(order):
-        lax.fori_loop(1, ctx, lambda d, _: (gathered(order, d).wait_recv(), 0)[1], 0)
+        def arrived(d, _):
+            j = lax.rem(sibling + 2 * d, ctx)
+            carried(order, j, chips + d, sibling).wait_recv()
+            return 0
+
+        lax.fori_loop(0, chips, arrived, 0)
 
     def product(k, lanes):
         at = pl.ds(k * chunk, chunk)
@@ -123,14 +141,31 @@
     def lanes_of(b):
         return pl.ds(pl.multiple_of(b * LANES, LANES), LANES)
 
+    def spread_rows(ref, b):
+        every = ref.shape[1]
+        tall = jnp.concatenate([ref[...]] * groups, axis=0)
+        lane = lax.broadcasted_iota(jnp.int32, (groups, state, every), 2)
+        group = lax.broadcasted_iota(jnp.int32, (groups, state, every), 0)
+        first = (place * lane_blocks + b) * groups
+        chosen = jnp.where(lane == group + first, tall.reshape(groups, state, every), 0.0)
+        column = chosen.sum(axis=2, keepdims=True).reshape(modes, 1)
+        return jnp.broadcast_to(column, (modes, LANES))
+
+    def table_step(b, _):
+        rate = spread_rows(rates_ref, b)
+        columns[b] = rate
+        rate_rows[b] = rate.T[0:8, :]
+        gain_rows[b] = (spread_rows(residues_ref, b) * jnp.sqrt(2.0 * rate)).T[0:8, :]
+        return 0
+
     def rate_row(b):
-        return rates_ref[pl.ds(place * lane_blocks + b, 1), :]
+        return rate_rows[b, 0:1, :]
 
     def gain_row(b):
-        return residues_ref[pl.ds(place * lane_blocks + b, 1), :] * jnp.sqrt(2.0 * rate_row(b))
+        return gain_rows[b, 0:1, :]
 
     def rate_columns(b):
-        return jnp.broadcast_to(rate_row(b), (LANES, modes)).T
+        return columns[b]
 
     def rate_lanes(b):
         return (rate_columns(b) * gmask_ref[...]).reshape(groups, state, LANES).sum(0)
@@ -138,21 +173,19 @@
     def state_step(b, _):
         lanes = lanes_of(b)
         tau = lax.broadcasted_iota(jnp.int32, (modes, chunk), 1).astype(F32)
-        upper, lower = split(jnp.exp(-rate_columns(b) * (chunk - 1.0 - tau)))
+        fading = jnp.concatenate(split(jnp.exp(-rate_columns(b) * (chunk - 1.0 - tau))), axis=0)
         decay = jnp.exp(-rate_lanes(b) * float(chunk))
         gmask = gmask_ref[...]
+        fresh = dot(fading, jnp.concatenate([product(k, lanes) for k in range(chunks)], axis=1))
+        fresh = fresh[:modes] + fresh[modes:]
         total = jnp.zeros((state, LANES), F32)
         for k in range(chunks):
-            x = product(k, lanes)
-            fresh = (dot(upper, x) + dot(lower, x)) * gmask
             before[k, :, lanes] = total
-            total = total * decay + fresh.reshape(groups, state, LANES).sum(0)
+            new = fresh[:, k * LANES:(k + 1) * LANES] * gmask
+            total = total * decay + new.reshape(groups, state, LANES).sum(0)
         own[:, lanes] = total
         return 0
 
-    loads[0].wait()
-    loads[1].wait()
-    lax.fori_loop(0, lane_blocks, state_step, 0)
 
     def to_peer(d):
         return pltpu.make_async_remote_copy(
@@ -164,9 +197,7 @@
             src_ref=own, dst_ref=states.at[j], send_sem=state_send.at[0], recv_sem=state_recv.at[j],
             device_id={"ctx": j}, device_id_type=MESH)
 
-    lax.fori_loop(1, ctx - me, lambda d, _: (to_peer(d).start(), 0)[1], 0)
-
-    def taps_step(b):
+    def taps_step(b, _):
         row = lax.broadcasted_iota(jnp.int32, (chunk, modes), 0).astype(F32)
         col = lax.broadcasted_iota(jnp.int32, (modes, chunk), 1).astype(F32)
         middle = chunk / 2.0
@@ -174,10 +205,12 @@
         b_hi, b_lo = split(jnp.exp(rate_columns(b) * (col - middle)))
         causal = lax.broadcasted_iota(jnp.int32, (chunk, chunk), 0) >= lax.broadcasted_iota(
             jnp.int32, (chunk, chunk), 1)
+        a_hi, a_lo = split(jnp.concatenate([falling * smask_ref[g:g + 1, :] for g in range(groups)], axis=0))
+        tap = dot(jnp.concatenate([a_hi, a_lo, a_hi], axis=1), jnp.concatenate([b_hi, b_hi, b_lo], axis=0))
         for g in range(groups):
-            a_hi, a_lo = split(falling * smask_ref[g:g + 1, :])
-            tap = dot(a_hi, b_hi) + dot(a_lo, b_hi) + dot(a_hi, b_lo)
-            taps[b, :, g * chunk:(g + 1) * chunk] = jnp.where(causal, tap, 0.0).astype(BF16)
+            own_tap = jnp.where(causal, tap[g * chunk:(g + 1) * chunk], 0.0)
+            taps[b, :, g * chunk:(g + 1) * chunk] = own_tap.astype(BF16)
+        return 0
 
     def inside_step(b, first):
         lanes = lanes_of(b)
@@ -214,7 +247,6 @@
             gated[at, lanes] = (q_ref[at, lanes].astype(F32) * convolved.astype(F32)).astype(BF16)
 
     def early_inside(b, _):
-        taps_step(b)
         inside_step(b, 0)
         return 0
 
@@ -227,6 +259,14 @@
         carry_step(b, half)
         return 0
 
+    lax.fori_loop(0, lane_blocks, table_step, 0)
+    lax.fori_loop(0, lane_blocks, taps_step, 0)
+    loads[0].wait()
+    loads[1].wait()
+    loads[2].start()
+    loads[3].start()
+    lax.fori_loop(0, lane_blocks, state_step, 0)
+    lax.fori_loop(1, ctx - me, lambda d, _: (to_peer(d).start(), 0)[1], 0)
     lax.fori_loop(0, lane_blocks, early_inside, 0)
     lax.fori_loop(0, me, lambda j, _: (from_peer(j).wait_recv(), 0)[1], 0)
     loads[2].wait()
@@ -277,6 +317,8 @@
         def _():
             copy(buf.at[h, came, m], h, i, m).start()
 
+    steps = inner * tiles
+
     def early_step(t, _):
         i = t // tiles
         m = t % tiles
@@ -287,12 +329,15 @@
         def _():
             spread_block(t)
 
+        @pl.when(is_helper & (t >= steps - (tp - 1)))
+        def _():
+            relay_block(t - (steps - (tp - 1)))
+
         @pl.when(t < lane_blocks)
         def _():
             late_step(t, 0)
         return 0
 
-    steps = inner * tiles
     lax.fori_loop(0, steps, early_step, 0)
     lax.fori_loop(steps, max(steps, lane_blocks), late_step, 0)
 
@@ -393,7 +438,8 @@
     @pl.when(is_helper)
     def _():
         for order in range(tp - 1):
-            lax.fori_loop(1, ctx, lambda d, _: (spread(order, d).wait_send(), 0)[1], 0)
+            lax.fori_loop(1, chips, lambda d, _: (across(order, d).wait_send(), 0)[1], 0)
+            lax.fori_loop(0, chips, lambda d, _: (beside(order, d).wait_send(), 0)[1], 0)
 
 
 def on_device(ctx, tp, query, keys, values, residues, rates, w_out):
@@ -424,6 +470,9 @@
             pltpu.VMEM((block, width), BF16),
             pltpu.VMEM((block, width), BF16),
             pltpu.VMEM(w_out.shape, BF16),
+            pltpu.VMEM((lane_blocks, modes, LANES), F32),
+            pltpu.VMEM((lane_blocks, 8, modes), F32),
+            pltpu.VMEM((lane_blocks, 8, modes), F32),
             pltpu.VMEM((block, width), BF16),
             pltpu.VMEM((ctx, state, width), F32),
             pltpu.VMEM((state, width), F32),
@@ -450,11 +499,11 @@
             dma((2, inner, tiles)),
         ],
         compiler_params=pltpu.CompilerParams(
-            collective_id=0, has_side_effects=True, vmem_limit_bytes=56 * 2**20),
+            collective_id=0, has_side_effects=True, vmem_limit_bytes=50 * 2**20),
         cost_estimate=pl.CostEstimate(
             flops=4 * block * width * width * tp, bytes_accessed=24 * block * width, transcendentals=0),
         name="hyena_layer",
-    )(query, keys, values, w_out, rates.reshape(-1, modes), residues.reshape(-1, modes), gmask, smask)
+    )(query, keys, values, w_out, rates.T, residues.T, gmask, smask)
 
 
 def solution(mesh):

time: 131 us -> 128 us (0.977); the launches traced: 129 us -> 128 us
  local copies, waits for them, and re-layouts: 6.11 us -> 4.28 us
    reshape x2 -> x0, local copies, waits for them, and re-layouts: 1.4 us -> none  [the longest x1 0.71 us: on_device(): rates.reshape(-1, modes)]
    unnamed x3 -> x9, local copies, waits for them, and re-layouts: 4.71 us -> 4.28 us
where the time goes in v3:
time: 128 us
  Pallas kernels  123 us (96%)
  local copies, waits for them, and re-layouts  4.28 us (3%)
    pallas_call x1, Pallas kernels, on_device(): pl.pallas_call(functools.partial(layer_kernel, ctx, tp, tiles, state, chu...  123 us
    unnamed x9, local copies, waits for them, and re-layouts  4.28 us

profile of v3, /device:TPU:14, one launch (start us, length us, event | category | flops | bytes accessed | tf_op | source)
XLA Modules:
  0.0 127.7 jit_solution(10755470835929284484)
XLA Ops:
  0.0 0.0 copy-start
  0.0 0.7 copy-done
  0.7 0.0 copy-start.1
  0.7 0.7 copy-done.1
  1.4 0.0 copy-start.2
  1.4 0.8 copy-done.2
  2.3 0.0 copy-start.3
  2.3 0.7 copy-done.3
  3.0 123.5 %hyena_layer.1 = bf16[1024,1024]{1,0:T(8,128)(2,1)S(1)} custom-call(bf16[1024,1024]{1,0:T(8,128)(2,1)} %q_hbm.1, bf16[1024,1024]{1,0:T(8,128)(2,1)} %k_hbm.1, bf16[1024,1024]{1,0:T(8,128)(2,1)} %v_hbm.1, bf16[1024,4096]{1,0:T(8,128)(2,1)} %w_hbm.1, f32[16,256]{1,0:T(8,128)S(1)} %bitcast.2, f32[16,256]{1,0:T(8,128)S(1)} %bitcast.3, f32[128,128]{1,0:T(8,128)S(1)} %copy-done.2, ...), custom_call_target="tpu_custom_call" | custom-call | flops 17179869184 | bytes 25165824 | tf_op jit(solution)/shard_map/hyena_layer/pallas_call | solution.py:463
  126.4 1.3 %copy.10 = bf16[1024,1024]{1,0:T(8,128)(2,1)} copy(bf16[1024,1024]{1,0:T(8,128)(2,1)S(1)} %hyena_layer.1) | data formatting | bytes 4194304
Async XLA Ops:
  0.0 0.7 copy-start
  0.7 0.7 copy-start.1
  1.4 0.8 copy-start.2
  2.3 0.7 copy-start.3

commit v4 on v3

--- a/solution.py
+++ b/solution.py
@@ -3,7 +3,6 @@
 
 import jax
 import jax.numpy as jnp
-import numpy as np
 from jax import lax
 from jax.experimental import pallas as pl
 from jax.experimental.pallas import tpu as pltpu
@@ -11,6 +10,7 @@
 
 SHARE = 16
 LANES = 128
+SUBS = 4
 MESH = pl.DeviceIdType.MESH
 F32 = jnp.float32
 BF16 = jnp.bfloat16
@@ -25,17 +25,19 @@
     return jnp.dot(a, b, preferred_element_type=F32)
 
 
-def layer_kernel(ctx, tp, tiles, state, chunk, q_hbm, k_hbm, v_hbm, w_hbm, rates_ref, residues_ref, gmask_ref,
-                 smask_ref, out_ref, q_ref, k_ref, v_ref, w_ref, columns, rate_rows, gain_rows, gated, states, own, before,
-                 inside, wide, taps, carry, extra, right_buf, left_buf, stage, part, load_sem, state_send, state_recv, hop_send,
+def layer_kernel(ctx, tp, tiles, state, chunk, q_hbm, k_hbm, v_hbm, w_hbm, rates_hbm, residues_hbm,
+                 out_ref, rates_ref, residues_ref, gmask_ref, smask_ref, q_ref, k_ref, v_ref, w_ref, columns, rate_rows, gain_rows, gated, states, own, before,
+                 inside, wide, taps, carry, extra, right_buf, left_buf, stage, part, early_part, load_sem, state_send, state_recv, hop_send,
                  hop_recv, spread_send, spread_recv, right_send, right_recv, left_send, left_recv):
     block, width = out_ref.shape
     chunks = block // chunk
-    half = chunks // 2
+    span = chunks // 4
     lane_blocks = width // LANES
     groups = LANES // SHARE
     modes = groups * state
     rows = block // (2 * tiles)
+    subs = SUBS
+    some = rows // subs
     piece = width // ctx
     inner = tp - 2
     me = lax.axis_index("ctx")
@@ -46,9 +48,10 @@
     is_helper = (place == 1) | (far == 1)
 
     loads = [pltpu.make_async_copy(src, dst, load_sem.at[i]) for i, (src, dst) in enumerate(
-        [(k_hbm, k_ref), (v_hbm, v_ref), (q_hbm, q_ref), (w_hbm, w_ref)])]
-    loads[0].start()
-    loads[1].start()
+        [(k_hbm, k_ref), (v_hbm, v_ref), (q_hbm, q_ref), (w_hbm, w_ref), (rates_hbm, rates_ref),
+         (residues_hbm, residues_ref)])]
+    for at in (4, 5, 0, 1):
+        loads[at].start()
 
     barrier = pltpu.get_barrier_semaphore()
 
@@ -135,7 +138,7 @@
         lax.fori_loop(0, chips, arrived, 0)
 
     def product(k, lanes):
-        at = pl.ds(k * chunk, chunk)
+        at = pl.ds(pl.multiple_of(k * chunk, chunk), chunk)
         return (k_ref[at, lanes].astype(F32) * v_ref[at, lanes].astype(F32)).astype(BF16)
 
     def lanes_of(b):
@@ -214,10 +217,10 @@
 
     def inside_step(b, first):
         lanes = lanes_of(b)
-        xs = [product(first + k, lanes) for k in range(half)]
+        xs = [product(first + k, lanes) for k in range(span)]
         for g in range(groups):
             only = gmask_ref[g * state:g * state + 1, :].astype(BF16)
-            for k in range(half):
+            for k in range(span):
                 wide[g * chunk:(g + 1) * chunk, k * LANES:(k + 1) * LANES] = xs[k] * only
         inside[b] = dot(taps[b], wide[...])
 
@@ -228,9 +231,9 @@
         decay = jnp.exp(-rlane * float(chunk))
         reached = lax.fori_loop(
             0, me, lambda j, r: r * along + states[j, :, lanes], jnp.zeros((state, LANES), F32))
-        reached = reached * jnp.exp(-rlane * float(chunk * first))
+        reached = reached * jnp.exp(-rlane * (chunk * first).astype(F32))
         gmask = gmask_ref[...]
-        for k in range(half):
+        for k in range(span):
             entering = before[first + k, :, lanes] + reached
             reached = reached * decay
             hi, lo = split(jnp.concatenate([entering] * groups, axis=0) * gmask)
@@ -241,8 +244,8 @@
         row = lax.broadcasted_iota(jnp.int32, (chunk, modes), 0).astype(F32)
         hi, lo = split(gain_row(b) * jnp.exp(-rate_row(b) * (row + 1.0)))
         full = inside[b] + dot(jnp.concatenate([hi, lo, hi], axis=1), carry[...])
-        for k in range(half):
-            at = pl.ds((first + k) * chunk, chunk)
+        for k in range(span):
+            at = pl.ds(pl.multiple_of((first + k) * chunk, chunk), chunk)
             convolved = full[:, k * LANES:(k + 1) * LANES].astype(BF16)
             gated[at, lanes] = (q_ref[at, lanes].astype(F32) * convolved.astype(F32)).astype(BF16)
 
@@ -251,22 +254,35 @@
         return 0
 
     def early_carry(b, _):
-        carry_step(b, 0)
-        return 0
-
-    def late_step(b, _):
-        inside_step(b, half)
-        carry_step(b, half)
-        return 0
-
+        carry_step(b, jnp.int32(0))
+        return 0
+
+    rest = 3 * lane_blocks
+    batch = max(1, lane_blocks // 2)
+
+    def late_step(item, _):
+        b = item % lane_blocks
+        first = (1 + item // lane_blocks) * span
+        inside_step(b, first)
+        carry_step(b, first)
+        return 0
+
+    group = lax.broadcasted_iota(jnp.int32, (groups, state, LANES), 0) * SHARE
+    lane = lax.broadcasted_iota(jnp.int32, (groups, state, LANES), 2)
+    gmask_ref[...] = jnp.where((lane >= group) & (lane < group + SHARE), 1.0, 0.0).reshape(modes, LANES)
+    group = lax.broadcasted_iota(jnp.int32, (groups, modes), 0) * state
+    lane = lax.broadcasted_iota(jnp.int32, (groups, modes), 1)
+    smask_ref[...] = jnp.where((lane >= group) & (lane < group + state), 1.0, 0.0)
+    loads[4].wait()
+    loads[5].wait()
     lax.fori_loop(0, lane_blocks, table_step, 0)
-    lax.fori_loop(0, lane_blocks, taps_step, 0)
     loads[0].wait()
     loads[1].wait()
     loads[2].start()
     loads[3].start()
     lax.fori_loop(0, lane_blocks, state_step, 0)
     lax.fori_loop(1, ctx - me, lambda d, _: (to_peer(d).start(), 0)[1], 0)
+    lax.fori_loop(0, lane_blocks, taps_step, 0)
     lax.fori_loop(0, lane_blocks, early_inside, 0)
     lax.fori_loop(0, me, lambda j, _: (from_peer(j).wait_recv(), 0)[1], 0)
     loads[2].wait()
@@ -283,15 +299,24 @@
         cols = pl.ds(pl.multiple_of(dest * width, width), width)
         return dot(gated[tile, :], w_ref[:, cols])
 
-    def rightward(src, h, i, m):
+    def some_rows(u):
+        return pl.ds(pl.multiple_of(u * some, some), some)
+
+    def rightward(src, h, i, m, u):
         return pltpu.make_async_remote_copy(
-            src_ref=src, dst_ref=right_buf.at[h, i, m], send_sem=right_send.at[h, i, m],
-            recv_sem=right_recv.at[h, i, m], device_id={"tp": place + 1}, device_id_type=MESH)
-
-    def leftward(src, h, i, m):
+            src_ref=src, dst_ref=right_buf.at[h, i, m, some_rows(u)], send_sem=right_send.at[h, i, m, u],
+            recv_sem=right_recv.at[h, i, m, u], device_id={"tp": place + 1}, device_id_type=MESH)
+
+    def leftward(src, h, i, m, u):
         return pltpu.make_async_remote_copy(
-            src_ref=src, dst_ref=left_buf.at[h, i, m], send_sem=left_send.at[h, i, m],
-            recv_sem=left_recv.at[h, i, m], device_id={"tp": place - 1}, device_id_type=MESH)
+            src_ref=src, dst_ref=left_buf.at[h, i, m, some_rows(u)], send_sem=left_send.at[h, i, m, u],
+            recv_sem=left_recv.at[h, i, m, u], device_id={"tp": place - 1}, device_id_type=MESH)
+
+    def each(body):
+        lax.fori_loop(0, subs, lambda u, _: (body(u), 0)[1], 0)
+
+    def received(copy, buf, h, i, m, u):
+        copy(buf.at[h, i, m, some_rows(u)], h, i, m, u).wait_recv()
 
     flows = ((place, rightward, right_buf, lambda d: d), (far, leftward, left_buf, lambda d: tp - 1 - d))
 
@@ -306,16 +331,18 @@
 
         @pl.when(go & (role > 0))
         def _():
-            copy(buf.at[h, came, m], h, came, m).wait_recv()
-            buf[h, came, m] = (part[...] + buf[h, came, m].astype(F32)).astype(BF16)
+            def add(u):
+                at = some_rows(u)
+                received(copy, buf, h, came, m, u)
+                buf[h, came, m, at] = (part[at, :] + buf[h, came, m, at].astype(F32)).astype(BF16)
+                copy(buf.at[h, came, m, at], h, i, m, u).start()
+
+            each(add)
 
         @pl.when(go & (role == 0))
         def _():
             buf[h, came, m] = part[...].astype(BF16)
-
-        @pl.when(go)
-        def _():
-            copy(buf.at[h, came, m], h, i, m).start()
+            each(lambda u: copy(buf.at[h, came, m, some_rows(u)], h, i, m, u).start())
 
     steps = inner * tiles
 
@@ -333,25 +360,27 @@
         def _():
             relay_block(t - (steps - (tp - 1)))
 
-        @pl.when(t < lane_blocks)
-        def _():
-            late_step(t, 0)
+        lax.fori_loop(jnp.minimum(t * batch, rest), jnp.minimum(t * batch + batch, rest), late_step, 0)
         return 0
 
     lax.fori_loop(0, steps, early_step, 0)
-    lax.fori_loop(steps, max(steps, lane_blocks), late_step, 0)
+    lax.fori_loop(min(steps * batch, rest), rest, late_step, 0)
 
     def end_step(flow, i, m):
         role, copy, buf, physical = flow
 
         @pl.when((role == 0) & (i == 0))
         def _():
-            copy(gated.at[late_tile(m)], 1, 0, m).start()
+            def send(u):
+                at = pl.ds(pl.multiple_of((tiles + m) * rows + u * some, some), some)
+                copy(gated.at[at], 1, 0, m, u).start()
+
+            each(send)
 
         @pl.when((role == 0) & (i == 1))
         def _():
             buf[1, 1, m] = share(early_tile(m), physical(1)).astype(BF16)
-            copy(buf.at[1, 1, m], 1, 1, m).start()
+            each(lambda u: copy(buf.at[1, 1, m, some_rows(u)], 1, 1, m, u).start())
 
     def helper_step(flow, i, m):
         role, copy, buf, physical = flow
@@ -362,14 +391,14 @@
 
             @pl.when(i == 0)
             def _():
-                copy(buf.at[1, 0, m], 1, 0, m).wait_recv()
+                each(lambda u: received(copy, buf, 1, 0, m, u))
 
             @pl.when(m == 0)
             def _():
                 await_block(i)
 
             stage[i, m] = (part[...] + dot(buf[1, 0, m], extra[column_block(i, place == 1)])).astype(BF16)
-            copy(stage.at[i, m], 1, i, m).start()
+            each(lambda u: copy(stage.at[i, m, some_rows(u)], 1, i, m, u).start())
 
     def late_sums(t, _):
         i = t // tiles
@@ -388,30 +417,27 @@
 
     def last_step(m, _):
         part[...] = share(late_tile(m), place)
+        early_part[...] = share(early_tile(m), place)
         for role, copy, buf, _physical in flows:
             @pl.when(role == 1)
             def _():
                 part[...] += dot(buf[1, 0, m], extra[column_block(tp - 2, place == 1)])
 
-            @pl.when(role >= 2)
-            def _():
-                copy(buf.at[1, inner - 1, m], 1, inner - 1, m).wait_recv()
-                part[...] += buf[1, inner - 1, m].astype(F32)
-
-        out_ref[late_tile(m), :] = part[...].astype(BF16)
-        part[...] = share(early_tile(m), place)
         for role, copy, buf, _physical in flows:
             @pl.when(role == 1)
             def _():
-                copy(buf.at[1, 1, m], 1, 1, m).wait_recv()
-                part[...] += buf[1, 1, m].astype(F32)
+                each(lambda u: received(copy, buf, 1, 1, m, u))
+                early_part[...] += buf[1, 1, m].astype(F32)
 
             @pl.when(role >= 2)
             def _():
-                copy(buf.at[0, inner - 1, m], 0, inner - 1, m).wait_recv()
-                part[...] += buf[0, inner - 1, m].astype(F32)
-
-        out_ref[early_tile(m), :] = part[...].astype(BF16)
+                each(lambda u: received(copy, buf, 0, inner - 1, m, u))
+                early_part[...] += buf[0, inner - 1, m].astype(F32)
+                each(lambda u: received(copy, buf, 1, inner - 1, m, u))
+                part[...] += buf[1, inner - 1, m].astype(F32)
+
+        out_ref[late_tile(m), :] = part[...].astype(BF16)
+        out_ref[early_tile(m), :] = early_part[...].astype(BF16)
         return 0
 
     lax.fori_loop(0, tiles, last_step, 0)
@@ -425,7 +451,7 @@
 
                 @pl.when(early_end | ((role > 0) & (i >= role - 1)))
                 def _():
-                    copy(buf.at[h, i, m], h, i, m).wait_send()
+                    each(lambda u: copy(buf.at[h, i, m, some_rows(u)], h, i, m, u).wait_send())
         return 0
 
     lax.fori_loop(0, steps, sent_step, 0)
@@ -447,25 +473,26 @@
     state = rates.shape[1]
     chunk = math.gcd(block, LANES)
     chunks = block // chunk
-    half = chunks // 2
+    span = chunks // 4
     groups = LANES // SHARE
     modes = groups * state
     lane_blocks = width // LANES
     tiles = 4
     inner = tp - 2
     rows = block // (2 * tiles)
-    at_row = np.arange(modes) // state
-    gmask = jnp.asarray((at_row[:, None] == np.arange(LANES)[None, :] // SHARE).astype(np.float32))
-    smask = jnp.asarray((np.arange(groups)[:, None] == at_row[None, :]).astype(np.float32))
     vmem = pl.BlockSpec(memory_space=pltpu.VMEM)
-    hbm = pl.BlockSpec(memory_space=pl.ANY)
+    hbm = pl.BlockSpec(memory_space=pltpu.HBM)
     dma = pltpu.SemaphoreType.DMA
     return pl.pallas_call(
         functools.partial(layer_kernel, ctx, tp, tiles, state, chunk),
         out_shape=jax.ShapeDtypeStruct((block, width), BF16),
-        in_specs=[hbm] * 4 + [vmem] * 4,
+        in_specs=[hbm] * 6,
         out_specs=vmem,
         scratch_shapes=[
+            pltpu.VMEM((state, rates.shape[0]), F32),
+            pltpu.VMEM((state, rates.shape[0]), F32),
+            pltpu.VMEM((modes, LANES), F32),
+            pltpu.VMEM((groups, modes), F32),
             pltpu.VMEM((block, width), BF16),
             pltpu.VMEM((block, width), BF16),
             pltpu.VMEM((block, width), BF16),
@@ -477,33 +504,34 @@
             pltpu.VMEM((ctx, state, width), F32),
             pltpu.VMEM((state, width), F32),
             pltpu.VMEM((chunks, state, width), F32),
-            pltpu.VMEM((lane_blocks, chunk, half * LANES), F32),
-            pltpu.VMEM((groups * chunk, half * LANES), BF16),
+            pltpu.VMEM((lane_blocks, chunk, span * LANES), F32),
+            pltpu.VMEM((groups * chunk, span * LANES), BF16),
             pltpu.VMEM((lane_blocks, chunk, groups * chunk), BF16),
-            pltpu.VMEM((3 * modes, half * LANES), BF16),
+            pltpu.VMEM((3 * modes, span * LANES), BF16),
             pltpu.VMEM((tp - 1, width, width), BF16),
             pltpu.VMEM((2, inner, tiles, rows, width), BF16),
             pltpu.VMEM((2, inner, tiles, rows, width), BF16),
             pltpu.VMEM((inner, tiles, rows, width), BF16),
             pltpu.VMEM((rows, width), F32),
-            dma((4,)),
+            pltpu.VMEM((rows, width), F32),
+            dma((6,)),
             dma((ctx,)),
             dma((ctx,)),
             dma((tp - 1,)),
             dma((tp - 1,)),
             dma((tp - 1, ctx)),
             dma((tp - 1, ctx)),
-            dma((2, inner, tiles)),
-            dma((2, inner, tiles)),
-            dma((2, inner, tiles)),
-            dma((2, inner, tiles)),
+            dma((2, inner, tiles, SUBS)),
+            dma((2, inner, tiles, SUBS)),
+            dma((2, inner, tiles, SUBS)),
+            dma((2, inner, tiles, SUBS)),
         ],
         compiler_params=pltpu.CompilerParams(
             collective_id=0, has_side_effects=True, vmem_limit_bytes=50 * 2**20),
         cost_estimate=pl.CostEstimate(
             flops=4 * block * width * width * tp, bytes_accessed=24 * block * width, transcendentals=0),
         name="hyena_layer",
-    )(query, keys, values, w_out, rates.T, residues.T, gmask, smask)
+    )(query, keys, values, w_out, rates.T, residues.T)
 
 
 def solution(mesh):

time: 128 us -> 128 us (level); the launches traced: 128 us -> 125 us
  local copies, waits for them, and re-layouts: 4.28 us -> 2.76 us
    unnamed x9 -> x5, local copies, waits for them, and re-layouts: 4.28 us -> 2.76 us
where the time goes in v4:
time: 128 us; the launch traced here: 125 us
  Pallas kernels  123 us (96%)
  local copies, waits for them, and re-layouts  2.76 us (2%)
    pallas_call x1, Pallas kernels, on_device(): pl.pallas_call(functools.partial(layer_kernel, ctx, tp, tiles, state, chu...  123 us
    unnamed x5, local copies, waits for them, and re-layouts  2.76 us

profile of v4, /device:TPU:14, one launch (start us, length us, event | category | flops | bytes accessed | tf_op | source)
XLA Modules:
  0.0 125.3 jit_solution(1644297241913774247)
XLA Ops:
  0.0 0.0 copy-start
  0.0 0.7 copy-done
  0.7 0.0 copy-start.1
  0.7 0.7 copy-done.1
  1.4 122.5 %hyena_layer.1 = bf16[1024,1024]{1,0:T(8,128)(2,1)S(1)} custom-call(bf16[1024,1024]{1,0:T(8,128)(2,1)} %q_hbm.1, bf16[1024,1024]{1,0:T(8,128)(2,1)} %k_hbm.1, bf16[1024,1024]{1,0:T(8,128)(2,1)} %v_hbm.1, bf16[1024,4096]{1,0:T(8,128)(2,1)} %w_hbm.1, f32[16,256]{1,0:T(8,128)S(1)} %bitcast.2, f32[16,256]{1,0:T(8,128)S(1)} %bitcast.3), custom_call_target="tpu_custom_call" | custom-call | flops 17179869184 | bytes 25165824 | tf_op jit(solution)/shard_map/hyena_layer/pallas_call | solution.py:486
  124.0 1.3 %copy.8 = bf16[1024,1024]{1,0:T(8,128)(2,1)} copy(bf16[1024,1024]{1,0:T(8,128)(2,1)S(1)} %hyena_layer.1) | data formatting | bytes 4194304
Async XLA Ops:
  0.0 0.7 copy-start
  0.7 0.7 copy-start.1

commit v5 on v4

--- a/solution.py
+++ b/solution.py
@@ -25,9 +25,9 @@
     return jnp.dot(a, b, preferred_element_type=F32)
 
 
-def layer_kernel(ctx, tp, tiles, state, chunk, q_hbm, k_hbm, v_hbm, w_hbm, rates_hbm, residues_hbm,
+def layer_kernel(ctx, tp, early, late, state, chunk, q_hbm, k_hbm, v_hbm, w_hbm, rates_hbm, residues_hbm,
                  out_ref, rates_ref, residues_ref, gmask_ref, smask_ref, q_ref, k_ref, v_ref, w_ref, columns, rate_rows, gain_rows, gated, states, own, before,
-                 inside, wide, taps, carry, extra, right_buf, left_buf, stage, part, early_part, load_sem, state_send, state_recv, hop_send,
+                 inside, wide, taps, carry, extra, right_buf, left_buf, stage, part, load_sem, state_send, state_recv, hop_send,
                  hop_recv, spread_send, spread_recv, right_send, right_recv, left_send, left_recv):
     block, width = out_ref.shape
     chunks = block // chunk
@@ -35,7 +35,7 @@
     lane_blocks = width // LANES
     groups = LANES // SHARE
     modes = groups * state
-    rows = block // (2 * tiles)
+    rows = block // (early + late)
     subs = SUBS
     some = rows // subs
     piece = width // ctx
@@ -91,7 +91,7 @@
 
     @pl.when((place == 0) | (far == 0))
     def _():
-        lax.fori_loop(0, tp - 1, hop_step, 0)
+        lax.fori_loop(0, inner, hop_step, 0)
 
     chips = ctx // 2
     sibling = me + 1 - 2 * lax.rem(me, 2)
@@ -289,38 +289,35 @@
     lax.fori_loop(0, lane_blocks, early_carry, 0)
     loads[3].wait()
 
-    def early_tile(m):
-        return pl.ds(pl.multiple_of(m * rows, rows), rows)
-
-    def late_tile(m):
-        return pl.ds(pl.multiple_of((tiles + m) * rows, rows), rows)
+    def tile_rows(tile):
+        return pl.ds(pl.multiple_of(tile * rows, rows), rows)
 
     def share(tile, dest):
         cols = pl.ds(pl.multiple_of(dest * width, width), width)
-        return dot(gated[tile, :], w_ref[:, cols])
+        return dot(gated[tile_rows(tile), :], w_ref[:, cols])
 
     def some_rows(u):
         return pl.ds(pl.multiple_of(u * some, some), some)
 
-    def rightward(src, h, i, m, u):
+    def rightward(src, i, tile, u):
         return pltpu.make_async_remote_copy(
-            src_ref=src, dst_ref=right_buf.at[h, i, m, some_rows(u)], send_sem=right_send.at[h, i, m, u],
-            recv_sem=right_recv.at[h, i, m, u], device_id={"tp": place + 1}, device_id_type=MESH)
-
-    def leftward(src, h, i, m, u):
+            src_ref=src, dst_ref=right_buf.at[i, tile, some_rows(u)], send_sem=right_send.at[i, tile, u],
+            recv_sem=right_recv.at[i, tile, u], device_id={"tp": place + 1}, device_id_type=MESH)
+
+    def leftward(src, i, tile, u):
         return pltpu.make_async_remote_copy(
-            src_ref=src, dst_ref=left_buf.at[h, i, m, some_rows(u)], send_sem=left_send.at[h, i, m, u],
-            recv_sem=left_recv.at[h, i, m, u], device_id={"tp": place - 1}, device_id_type=MESH)
+            src_ref=src, dst_ref=left_buf.at[i, tile, some_rows(u)], send_sem=left_send.at[i, tile, u],
+            recv_sem=left_recv.at[i, tile, u], device_id={"tp": place - 1}, device_id_type=MESH)
 
     def each(body):
         lax.fori_loop(0, subs, lambda u, _: (body(u), 0)[1], 0)
 
-    def received(copy, buf, h, i, m, u):
-        copy(buf.at[h, i, m, some_rows(u)], h, i, m, u).wait_recv()
+    def received(copy, buf, i, tile):
+        each(lambda u: copy(buf.at[i, tile, some_rows(u)], i, tile, u).wait_recv())
 
     flows = ((place, rightward, right_buf, lambda d: d), (far, leftward, left_buf, lambda d: tp - 1 - d))
 
-    def sums_step(flow, h, i, m, tile, go):
+    def sums_step(flow, i, tile, go):
         role, copy, buf, physical = flow
         came = i - (role >= 2).astype(jnp.int32)
         dest = tp - 1 - i + jnp.maximum(role - 1, 0)
@@ -333,32 +330,32 @@
         def _():
             def add(u):
                 at = some_rows(u)
-                received(copy, buf, h, came, m, u)
-                buf[h, came, m, at] = (part[at, :] + buf[h, came, m, at].astype(F32)).astype(BF16)
-                copy(buf.at[h, came, m, at], h, i, m, u).start()
+                copy(buf.at[came, tile, at], came, tile, u).wait_recv()
+                buf[came, tile, at] = (part[at, :] + buf[came, tile, at].astype(F32)).astype(BF16)
+                copy(buf.at[came, tile, at], i, tile, u).start()
 
             each(add)
 
         @pl.when(go & (role == 0))
         def _():
-            buf[h, came, m] = part[...].astype(BF16)
-            each(lambda u: copy(buf.at[h, came, m, some_rows(u)], h, i, m, u).start())
-
-    steps = inner * tiles
+            buf[came, tile] = part[...].astype(BF16)
+            each(lambda u: copy(buf.at[came, tile, some_rows(u)], i, tile, u).start())
+
+    steps = early * inner
 
     def early_step(t, _):
-        i = t // tiles
-        m = t % tiles
+        m = t // inner
+        i = t % inner
         for flow in flows:
-            sums_step(flow, 0, i, m, early_tile(m), i >= flow[0] - 1)
-
-        @pl.when(is_helper & (t < tp - 1))
+            sums_step(flow, i, m, i >= flow[0] - 1)
+
+        @pl.when(is_helper & (t < inner))
         def _():
             spread_block(t)
 
-        @pl.when(is_helper & (t >= steps - (tp - 1)))
-        def _():
-            relay_block(t - (steps - (tp - 1)))
+        @pl.when(is_helper & (t >= steps - inner))
+        def _():
+            relay_block(t - (steps - inner))
 
         lax.fori_loop(jnp.minimum(t * batch, rest), jnp.minimum(t * batch + batch, rest), late_step, 0)
         return 0
@@ -366,95 +363,119 @@
     lax.fori_loop(0, steps, early_step, 0)
     lax.fori_loop(min(steps * batch, rest), rest, late_step, 0)
 
-    def end_step(flow, i, m):
+    def end_step(flow, m, i, to_right):
         role, copy, buf, physical = flow
+        tile = early + m
 
         @pl.when((role == 0) & (i == 0))
         def _():
             def send(u):
-                at = pl.ds(pl.multiple_of((tiles + m) * rows + u * some, some), some)
-                copy(gated.at[at], 1, 0, m, u).start()
+                at = pl.ds(pl.multiple_of(tile * rows + u * some, some), some)
+                copy(gated.at[at], 0, tile, u).start()
 
             each(send)
 
-        @pl.when((role == 0) & (i == 1))
-        def _():
-            buf[1, 1, m] = share(early_tile(m), physical(1)).astype(BF16)
-            each(lambda u: copy(buf.at[1, 1, m, some_rows(u)], 1, 1, m, u).start())
-
-    def helper_step(flow, i, m):
+        @pl.when((role == 0) & (i == 1) & (m == 0))
+        def _():
+            hop(tp - 2, to_right).start()
+
+        @pl.when((role == 0) & (i == 1) & (m > 0) & (m <= early))
+        def _():
+            buf[1, tile] = share(m - 1, physical(1)).astype(BF16)
+            each(lambda u: copy(buf.at[1, tile, some_rows(u)], 1, tile, u).start())
+
+    def helper_step(flow, m, i):
         role, copy, buf, physical = flow
+        tile = early + m
 
         @pl.when(role == 1)
         def _():
-            part[...] = share(late_tile(m), physical(tp - 1 - i))
+            part[...] = share(tile, physical(tp - 1 - i))
 
             @pl.when(i == 0)
             def _():
-                each(lambda u: received(copy, buf, 1, 0, m, u))
+                received(copy, buf, 0, tile)
 
             @pl.when(m == 0)
             def _():
                 await_block(i)
 
-            stage[i, m] = (part[...] + dot(buf[1, 0, m], extra[column_block(i, place == 1)])).astype(BF16)
-            each(lambda u: copy(stage.at[i, m, some_rows(u)], 1, i, m, u).start())
+            stage[i, m] = (part[...] + dot(buf[0, tile], extra[column_block(i, place == 1)])).astype(BF16)
+            each(lambda u: copy(stage.at[i, m, some_rows(u)], i, tile, u).start())
 
     def late_sums(t, _):
-        i = t // tiles
-        m = t % tiles
-        for flow in flows:
-            end_step(flow, i, m)
-            helper_step(flow, i, m)
-            sums_step(flow, 1, i, m, late_tile(m), (flow[0] >= 2) & (i >= flow[0] - 1))
-        return 0
-
-    lax.fori_loop(0, steps, late_sums, 0)
+        m = t // inner
+        i = t % inner
+        for flow, to_right in zip(flows, (True, False)):
+            end_step(flow, m, i, to_right)
+            helper_step(flow, m, i)
+            sums_step(flow, i, early + m, (flow[0] >= 2) & (i >= flow[0] - 1))
+
+        @pl.when(is_helper & (i == inner - 1) & (m == 1))
+        def _():
+            spread_block(tp - 2)
+
+        @pl.when(is_helper & (i == inner - 1) & (m == late - 2))
+        def _():
+            relay_block(tp - 2)
+        return 0
+
+    lax.fori_loop(0, late * inner, late_sums, 0)
+
+    def early_result(m, _):
+        part[...] = share(m, place)
+        for role, copy, buf, _physical in flows:
+            @pl.when(role == 1)
+            def _():
+                received(copy, buf, 1, early + 1 + m)
+                part[...] += buf[1, early + 1 + m].astype(F32)
+
+            @pl.when(role >= 2)
+            def _():
+                received(copy, buf, inner - 1, m)
+                part[...] += buf[inner - 1, m].astype(F32)
+
+        out_ref[tile_rows(m), :] = part[...].astype(BF16)
+        return 0
+
+    lax.fori_loop(0, early, early_result, 0)
 
     @pl.when(is_helper)
     def _():
         await_block(tp - 2)
 
-    def last_step(m, _):
-        part[...] = share(late_tile(m), place)
-        early_part[...] = share(early_tile(m), place)
+    def late_result(m, _):
+        tile = early + m
+        part[...] = share(tile, place)
         for role, copy, buf, _physical in flows:
             @pl.when(role == 1)
             def _():
-                part[...] += dot(buf[1, 0, m], extra[column_block(tp - 2, place == 1)])
+                part[...] += dot(buf[0, tile], extra[column_block(tp - 2, place == 1)])
 
         for role, copy, buf, _physical in flows:
-            @pl.when(role == 1)
-            def _():
-                each(lambda u: received(copy, buf, 1, 1, m, u))
-                early_part[...] += buf[1, 1, m].astype(F32)
-
             @pl.when(role >= 2)
             def _():
-                each(lambda u: received(copy, buf, 0, inner - 1, m, u))
-                early_part[...] += buf[0, inner - 1, m].astype(F32)
-                each(lambda u: received(copy, buf, 1, inner - 1, m, u))
-                part[...] += buf[1, inner - 1, m].astype(F32)
-
-        out_ref[late_tile(m), :] = part[...].astype(BF16)
-        out_ref[early_tile(m), :] = early_part[...].astype(BF16)
-        return 0
-
-    lax.fori_loop(0, tiles, last_step, 0)
+                received(copy, buf, inner - 1, tile)
+                part[...] += buf[inner - 1, tile].astype(F32)
+
+        out_ref[tile_rows(tile), :] = part[...].astype(BF16)
+        return 0
+
+    lax.fori_loop(0, late, late_result, 0)
 
     def sent_step(t, _):
-        i = t // tiles
-        m = t % tiles
+        tile = t // inner
+        i = t % inner
+        m = tile - early
         for role, copy, buf, _physical in flows:
-            for h in range(2):
-                early_end = (role == 0) if h == 0 else (role == 0) & (i < 2)
-
-                @pl.when(early_end | ((role > 0) & (i >= role - 1)))
-                def _():
-                    each(lambda u: copy(buf.at[h, i, m, some_rows(u)], h, i, m, u).wait_send())
-        return 0
-
-    lax.fori_loop(0, steps, sent_step, 0)
+            from_end = (m < 0) | (i == 0) | ((i == 1) & (m > 0) & (m <= early))
+
+            @pl.when(((role == 0) & from_end) | ((role > 0) & (i >= role - 1)))
+            def _():
+                each(lambda u: copy(buf.at[i, tile, some_rows(u)], i, tile, u).wait_send())
+        return 0
+
+    lax.fori_loop(0, (early + late) * inner, sent_step, 0)
     lax.fori_loop(1, ctx - me, lambda d, _: (to_peer(d).wait_send(), 0)[1], 0)
 
     @pl.when((place == 0) | (far == 0))
@@ -477,14 +498,14 @@
     groups = LANES // SHARE
     modes = groups * state
     lane_blocks = width // LANES
-    tiles = 4
+    early, late = 3, 5
     inner = tp - 2
-    rows = block // (2 * tiles)
+    rows = block // (early + late)
     vmem = pl.BlockSpec(memory_space=pltpu.VMEM)
     hbm = pl.BlockSpec(memory_space=pltpu.HBM)
     dma = pltpu.SemaphoreType.DMA
     return pl.pallas_call(
-        functools.partial(layer_kernel, ctx, tp, tiles, state, chunk),
+        functools.partial(layer_kernel, ctx, tp, early, late, state, chunk),
         out_shape=jax.ShapeDtypeStruct((block, width), BF16),
         in_specs=[hbm] * 6,
         out_specs=vmem,
@@ -509,10 +530,9 @@
             pltpu.VMEM((lane_blocks, chunk, groups * chunk), BF16),
             pltpu.VMEM((3 * modes, span * LANES), BF16),
             pltpu.VMEM((tp - 1, width, width), BF16),
-            pltpu.VMEM((2, inner, tiles, rows, width), BF16),
-            pltpu.VMEM((2, inner, tiles, rows, width), BF16),
-            pltpu.VMEM((inner, tiles, rows, width), BF16),
-            pltpu.VMEM((rows, width), F32),
+            pltpu.VMEM((inner, early + late, rows, width), BF16),
+            pltpu.VMEM((inner, early + late, rows, width), BF16),
+            pltpu.VMEM((inner, late, rows, width), BF16),
             pltpu.VMEM((rows, width), F32),
             dma((6,)),
             dma((ctx,)),
@@ -521,10 +541,10 @@
             dma((tp - 1,)),
             dma((tp - 1, ctx)),
             dma((tp - 1, ctx)),
-            dma((2, inner, tiles, SUBS)),
-            dma((2, inner, tiles, SUBS)),
-            dma((2, inner, tiles, SUBS)),
-            dma((2, inner, tiles, SUBS)),
+            dma((inner, early + late, SUBS)),
+            dma((inner, early + late, SUBS)),
+            dma((inner, early + late, SUBS)),
+            dma((inner, early + late, SUBS)),
         ],
         compiler_params=pltpu.CompilerParams(
             collective_id=0, has_side_effects=True, vmem_limit_bytes=50 * 2**20),

time: 128 us -> 129 us (level); the launches traced: 125 us -> 128 us
  Pallas kernels: 123 us -> 126 us
    pallas_call x1, Pallas kernels: 123 us -> 126 us  [on_device(): pl.pallas_call(functools.partial(layer_kernel, ctx, tp, early, late, stat...]
where the time goes in v5:
time: 129 us; the launch traced here: 128 us
  Pallas kernels  126 us (98%)
  local copies, waits for them, and re-layouts  2.76 us (2%)
    pallas_call x1, Pallas kernels, on_device(): pl.pallas_call(functools.partial(layer_kernel, ctx, tp, early, late, stat...  126 us
    unnamed x5, local copies, waits for them, and re-layouts  2.76 us

profile of v5, /device:TPU:14, one launch (start us, length us, event | category | flops | bytes accessed | tf_op | source)
XLA Modules:
  0.0 128.3 jit_solution(4414846138654689663)
XLA Ops:
  0.0 0.0 copy-start
  0.0 0.7 copy-done
  0.7 0.0 copy-start.1
  0.7 0.7 copy-done.1
  1.4 125.6 %hyena_layer.1 = bf16[1024,1024]{1,0:T(8,128)(2,1)S(1)} custom-call(bf16[1024,1024]{1,0:T(8,128)(2,1)} %q_hbm.1, bf16[1024,1024]{1,0:T(8,128)(2,1)} %k_hbm.1, bf16[1024,1024]{1,0:T(8,128)(2,1)} %v_hbm.1, bf16[1024,4096]{1,0:T(8,128)(2,1)} %w_hbm.1, f32[16,256]{1,0:T(8,128)S(1)} %bitcast.2, f32[16,256]{1,0:T(8,128)S(1)} %bitcast.3), custom_call_target="tpu_custom_call" | custom-call | flops 17179869184 | bytes 25165824 | tf_op jit(solution)/shard_map/hyena_layer/pallas_call | solution.py:507
  127.0 1.3 %copy.8 = bf16[1024,1024]{1,0:T(8,128)(2,1)} copy(bf16[1024,1024]{1,0:T(8,128)(2,1)S(1)} %hyena_layer.1) | data formatting | bytes 4194304
Async XLA Ops:
  0.0 0.7 copy-start
  0.7 0.7 copy-start.1

commit v6 on v4

--- a/solution.py
+++ b/solution.py
@@ -10,7 +10,7 @@
 
 SHARE = 16
 LANES = 128
-SUBS = 4
+SUBS = 8
 MESH = pl.DeviceIdType.MESH
 F32 = jnp.float32
 BF16 = jnp.bfloat16
@@ -258,7 +258,7 @@
         return 0
 
     rest = 3 * lane_blocks
-    batch = max(1, lane_blocks // 2)
+    batch = lane_blocks
 
     def late_step(item, _):
         b = item % lane_blocks
@@ -477,7 +477,7 @@
     groups = LANES // SHARE
     modes = groups * state
     lane_blocks = width // LANES
-    tiles = 4
+    tiles = 2
     inner = tp - 2
     rows = block // (2 * tiles)
     vmem = pl.BlockSpec(memory_space=pltpu.VMEM)

time: 128 us -> 133 us (1.039)
  Pallas kernels: 123 us -> 128 us
    pallas_call x1, Pallas kernels: 123 us -> 128 us  [on_device(): pl.pallas_call(functools.partial(layer_kernel, ctx, tp, tiles, state, chu...]
where the time goes in v6:
time: 133 us; the launch traced here: 131 us
  Pallas kernels  128 us (96%)
  local copies, waits for them, and re-layouts  2.76 us (2%)
    pallas_call x1, Pallas kernels, on_device(): pl.pallas_call(functools.partial(layer_kernel, ctx, tp, tiles, state, chu...  128 us
    unnamed x5, local copies, waits for them, and re-layouts  2.76 us

profile of v6, /device:TPU:14, one launch (start us, length us, event | category | flops | bytes accessed | tf_op | source)
XLA Modules:
  0.0 131.2 jit_solution(15150292371707824035)
XLA Ops:
  0.0 0.0 copy-start
  0.0 0.7 copy-done
  0.7 0.0 copy-start.1
  0.7 0.7 copy-done.1
  1.4 128.4 %hyena_layer.1 = bf16[1024,1024]{1,0:T(8,128)(2,1)S(1)} custom-call(bf16[1024,1024]{1,0:T(8,128)(2,1)} %q_hbm.1, bf16[1024,1024]{1,0:T(8,128)(2,1)} %k_hbm.1, bf16[1024,1024]{1,0:T(8,128)(2,1)} %v_hbm.1, bf16[1024,4096]{1,0:T(8,128)(2,1)} %w_hbm.1, f32[16,256]{1,0:T(8,128)S(1)} %bitcast.2, f32[16,256]{1,0:T(8,128)S(1)} %bitcast.3), custom_call_target="tpu_custom_call" | custom-call | flops 17179869184 | bytes 25165824 | tf_op jit(solution)/shard_map/hyena_layer/pallas_call | solution.py:486
  129.8 1.3 %copy.8 = bf16[1024,1024]{1,0:T(8,128)(2,1)} copy(bf16[1024,1024]{1,0:T(8,128)(2,1)S(1)} %hyena_layer.1) | data formatting | bytes 4194304
Async XLA Ops:
  0.0 0.7 copy-start
  0.7 0.7 copy-start.1

commit v7 on v4

--- a/solution.py
+++ b/solution.py
@@ -10,7 +10,7 @@
 
 SHARE = 16
 LANES = 128
-SUBS = 4
+SUBS = 2
 MESH = pl.DeviceIdType.MESH
 F32 = jnp.float32
 BF16 = jnp.bfloat16
@@ -477,7 +477,7 @@
     groups = LANES // SHARE
     modes = groups * state
     lane_blocks = width // LANES
-    tiles = 4
+    tiles = 8
     inner = tp - 2
     rows = block // (2 * tiles)
     vmem = pl.BlockSpec(memory_space=pltpu.VMEM)

time: 128 us -> 125 us (0.977); the launches traced: 125 us -> 124 us
  Pallas kernels: 123 us -> 121 us
    pallas_call x1, Pallas kernels: 123 us -> 121 us  [on_device(): pl.pallas_call(functools.partial(layer_kernel, ctx, tp, tiles, state, chu...]
where the time goes in v7:
time: 125 us; the launch traced here: 124 us
  Pallas kernels  121 us (97%)
  local copies, waits for them, and re-layouts  2.76 us (2%)
    pallas_call x1, Pallas kernels, on_device(): pl.pallas_call(functools.partial(layer_kernel, ctx, tp, tiles, state, chu...  121 us
    unnamed x5, local copies, waits for them, and re-layouts  2.76 us

profile of v7, /device:TPU:14, one launch (start us, length us, event | category | flops | bytes accessed | tf_op | source)
XLA Modules:
  0.0 123.7 jit_solution(13777384479579674080)
XLA Ops:
  0.0 0.0 copy-start
  0.0 0.7 copy-done
  0.7 0.0 copy-start.1
  0.7 0.7 copy-done.1
  1.4 121.0 %hyena_layer.1 = bf16[1024,1024]{1,0:T(8,128)(2,1)S(1)} custom-call(bf16[1024,1024]{1,0:T(8,128)(2,1)} %q_hbm.1, bf16[1024,1024]{1,0:T(8,128)(2,1)} %k_hbm.1, bf16[1024,1024]{1,0:T(8,128)(2,1)} %v_hbm.1, bf16[1024,4096]{1,0:T(8,128)(2,1)} %w_hbm.1, f32[16,256]{1,0:T(8,128)S(1)} %bitcast.2, f32[16,256]{1,0:T(8,128)S(1)} %bitcast.3), custom_call_target="tpu_custom_call" | custom-call | flops 17179869184 | bytes 25165824 | tf_op jit(solution)/shard_map/hyena_layer/pallas_call | solution.py:486
  122.4 1.3 %copy.8 = bf16[1024,1024]{1,0:T(8,128)(2,1)} copy(bf16[1024,1024]{1,0:T(8,128)(2,1)S(1)} %hyena_layer.1) | data formatting | bytes 4194304
Async XLA Ops:
  0.0 0.7 copy-start
  0.7 0.7 copy-start.1
